TPU v7x, 512 devices: a whole 4x4x16 slice. The times are simulated.
512 devices in a mesh: ctx: 32 (over z, x_lo), ch: 16 (over y, x_hi, core).
Axes of the slice: x: 4 (x_hi: 2, x_lo: 2; x = x_hi * 2 + x_lo), y: 4, z: 16, core: 2. Of those that a mesh axis runs over, the one named last changes fastest.
Arguments:
- query: bfloat16 [4096, 4096], P('ch', 'ctx'), may hold values from -6 to 6
- key_gate: bfloat16 [4096, 4096], P('ch', 'ctx'), may hold values from -6 to 6
- value_in: bfloat16 [4096, 4096], P('ch', 'ctx'), may hold values from -6 to 6
- grad_output: bfloat16 [4096, 4096], P('ch', 'ctx'), may hold values from -6 to 6
- residue: float32 [4096, 16], P('ch'), may hold values from -4 to 4
- log_rate: float32 [4096, 16], P('ch'), may hold values from -1.386 to 6.685
Outputs:
- grad_query: bfloat16 [4096, 4096], P('ch', 'ctx')
- grad_key: bfloat16 [4096, 4096], P('ch', 'ctx')
- grad_value: bfloat16 [4096, 4096], P('ch', 'ctx')
- grad_residue: float32 [4096, 16], P('ch')
- grad_log_rate: float32 [4096, 16], P('ch')
All inputs are finite; a program needn't handle non-finite values.
Results may differ from a plain program's by a relative error of at most 0.0122.
Values may be sent and summed in bfloat16 or wider, within the bound.
No kernel may reach another device: no remote copies, remote signals or barrier semaphores. Data moves between devices by JAX's collectives and lax.ppermute only.
A program may use at most 64 MiB of HBM per device.

v0:
```python
import math

import jax
import jax.numpy as jnp
from jax import lax
from jax.sharding import PartitionSpec as P

PRECISE = lax.Precision.HIGHEST


def pick_columns(length):
    candidate = 1
    while length % (candidate * 2) == 0 and candidate * 2 * (candidate * 2) <= 2 * length:
        candidate = candidate * 2
    return candidate


def dft_tables(count):
    indices = jnp.arange(count, dtype=jnp.int32)
    angle = (indices[:, None] * indices[None, :] % count).astype(jnp.float32) * (
        2.0 * math.pi / count
    )
    return (jnp.cos(angle), jnp.sin(angle))


def make_tables(length):
    columns = pick_columns(length)
    row_count = 2 * length // columns
    cos_rows, sin_rows = dft_tables(row_count)
    cos_cols, sin_cols = dft_tables(columns)
    row_index = jnp.arange(row_count, dtype=jnp.int32)
    col_index = jnp.arange(columns, dtype=jnp.int32)
    angle = (row_index[:, None] * col_index[None, :]).astype(jnp.float32) * (
        2.0 * math.pi / (2 * length)
    )
    return (cos_rows, sin_rows, cos_cols, sin_cols, jnp.cos(angle), jnp.sin(angle))


def forward_real(signal, tables):
    cos_rows, sin_rows, cos_cols, sin_cols, turn_cos, turn_sin = tables
    half_rows = cos_rows.shape[0] // 2
    blocks = signal.reshape(signal.shape[0], half_rows, cos_cols.shape[0])
    first_re = jnp.einsum("cab,af->cfb", blocks, cos_rows[:half_rows], precision=PRECISE)
    first_im = -jnp.einsum("cab,af->cfb", blocks, sin_rows[:half_rows], precision=PRECISE)
    turned_re = first_re * turn_cos + first_im * turn_sin
    turned_im = first_im * turn_cos - first_re * turn_sin
    out_re = jnp.einsum("cfb,bg->cfg", turned_re, cos_cols, precision=PRECISE) + jnp.einsum(
        "cfb,bg->cfg", turned_im, sin_cols, precision=PRECISE
    )
    out_im = jnp.einsum("cfb,bg->cfg", turned_im, cos_cols, precision=PRECISE) - jnp.einsum(
        "cfb,bg->cfg", turned_re, sin_cols, precision=PRECISE
    )
    return (out_re, out_im)


def inverse_real(spec_re, spec_im, tables):
    cos_rows, sin_rows, cos_cols, sin_cols, turn_cos, turn_sin = tables
    half_rows = cos_rows.shape[0] // 2
    back_re = jnp.einsum("cfg,gb->cfb", spec_re, cos_cols, precision=PRECISE) - jnp.einsum(
        "cfg,gb->cfb", spec_im, sin_cols, precision=PRECISE
    )
    back_im = jnp.einsum("cfg,gb->cfb", spec_re, sin_cols, precision=PRECISE) + jnp.einsum(
        "cfg,gb->cfb", spec_im, cos_cols, precision=PRECISE
    )
    turned_re = back_re * turn_cos - back_im * turn_sin
    turned_im = back_re * turn_sin + back_im * turn_cos
    values = jnp.einsum(
        "cfb,fa->cab", turned_re, cos_rows[:, :half_rows], precision=PRECISE
    ) - jnp.einsum("cfb,fa->cab", turned_im, sin_rows[:, :half_rows], precision=PRECISE)
    scale_back = 1.0 / (cos_rows.shape[0] * cos_cols.shape[0])
    return values.reshape(values.shape[0], -1) * scale_back


def times_spec(left, right, conj_right):
    left_re, left_im = left
    right_re, right_im = right
    if conj_right:
        right_im = -right_im
    return (left_re * right_re - left_im * right_im, left_re * right_im + left_im * right_re)


def filter_parts(residue_loc, log_loc, length):
    times = jnp.arange(length, dtype=jnp.float32)
    rates = jnp.exp(log_loc) / length
    exponent = rates[:, :, None] * times[None, None, :]
    decay_table = jnp.exp(-exponent)
    filt = jnp.einsum("cn,cnt->ct", residue_loc, decay_table, precision=PRECISE) * (
        1.0 / math.sqrt(length)
    )
    return (filt, decay_table, exponent)


def exchange_plan(mixed_input, grad_conv, residue, log_rate):
    ctx_count = lax.axis_size("ctx")
    chan_width = mixed_input.shape[0] // ctx_count
    length = mixed_input.shape[1] * ctx_count
    chan_start = lax.axis_index("ctx") * chan_width
    residue_loc = lax.dynamic_slice_in_dim(residue, chan_start, chan_width, 0)
    log_loc = lax.dynamic_slice_in_dim(log_rate, chan_start, chan_width, 0)
    tables = make_tables(length)
    filt, decay_table, exponent = filter_parts(residue_loc, log_loc, length)
    seq_mixed, seq_grad = (
        lax.all_to_all(mixed_input, "ctx", split_axis=0, concat_axis=1, tiled=True),
        lax.all_to_all(grad_conv, "ctx", split_axis=0, concat_axis=1, tiled=True),
    )
    filt_spec = forward_real(filt, tables)
    mixed_spec = forward_real(seq_mixed.astype(jnp.float32), tables)
    grad_spec = forward_real(seq_grad.astype(jnp.float32), tables)
    conv_spec = times_spec(mixed_spec, filt_spec, False)
    conv_seq = inverse_real(conv_spec[0], conv_spec[1], tables).astype(jnp.bfloat16)
    back_spec = times_spec(grad_spec, filt_spec, True)
    input_seq = inverse_real(back_spec[0], back_spec[1], tables).astype(jnp.bfloat16)
    conv_out, grad_mixed = (
        lax.all_to_all(conv_seq, "ctx", split_axis=1, concat_axis=0, tiled=True),
        lax.all_to_all(input_seq, "ctx", split_axis=1, concat_axis=0, tiled=True),
    )
    filt_grad_spec = times_spec(grad_spec, mixed_spec, True)
    filt_grad = inverse_real(filt_grad_spec[0], filt_grad_spec[1], tables)
    grad_res = jnp.einsum("ct,cnt->cn", filt_grad, decay_table, precision=PRECISE) / length
    grad_log = -(residue_loc / length) * jnp.einsum(
        "ct,cnt->cn", filt_grad, decay_table * exponent, precision=PRECISE
    )
    grad_residue, grad_log_rate = (
        lax.all_gather(grad_res, "ctx", axis=0, tiled=True),
        lax.all_gather(grad_log, "ctx", axis=0, tiled=True),
    )
    return (conv_out, grad_mixed, grad_residue, grad_log_rate)


def on_device(query, key_gate, value_in, grad_output, residue, log_rate):
    mixed_input = (key_gate.astype(jnp.float32) * value_in.astype(jnp.float32)).astype(jnp.bfloat16)
    grad_conv = (query.astype(jnp.float32) * grad_output.astype(jnp.float32)).astype(jnp.bfloat16)
    conv_out, grad_mixed, grad_residue, grad_log_rate = exchange_plan(
        mixed_input, grad_conv, residue, log_rate
    )
    grad_query = (grad_output.astype(jnp.float32) * conv_out.astype(jnp.float32)).astype(
        jnp.bfloat16
    )
    grad_key = (grad_mixed.astype(jnp.float32) * value_in.astype(jnp.float32)).astype(jnp.bfloat16)
    grad_value = (grad_mixed.astype(jnp.float32) * key_gate.astype(jnp.float32)).astype(
        jnp.bfloat16
    )
    return (grad_query, grad_key, grad_value, grad_residue, grad_log_rate)


def solution(mesh):
    return jax.shard_map(
        on_device,
        mesh=mesh,
        in_specs=(
            P("ch", "ctx"),
            P("ch", "ctx"),
            P("ch", "ctx"),
            P("ch", "ctx"),
            P("ch", None),
            P("ch", None),
        ),
        out_specs=(P("ch", "ctx"), P("ch", "ctx"), P("ch", "ctx"), P("ch", None), P("ch", None)),
        check_vma=False,
    )
```

profile of v0, /device:TPU:24, one launch (start us, length us, event | category | flops | bytes accessed | tf_op | source)
XLA Modules:
  0.0 217.8 jit_solution(7522058300477505718)
XLA Ops:
  0.7 1.5 fusion.74
  2.2 16.4 %all-to-all-start = ((bf16[32,8,128]{2,1,0:T(8,128)(2,1)}), bf16[32,8,128]{2,1,0:T(8,128)(2,1)S(1)}, u32[]{:S(2)}, u32[]{:S(2)}) async-start(bf16[32,8,128]{2,1,0:T(8,128)(2,1)} %fusion.74), calls=%async_computation | async-start | bytes 131072 | tf_op jit(solution)/shard_map/all_to_all | solution.py:103
  19.5 1.4 fusion.3
  22.0 0.6 fusion.21
  22.5 0.6 fusion.25
  23.1 0.6 convolution_subtract_fusion.7
  24.0 0.6 fusion.75
  24.6 0.6 convolution_add_fusion.4
  25.2 7.1 %all-to-all-done = bf16[32,8,128]{2,1,0:T(8,128)(2,1)S(1)} async-done(((bf16[32,8,128]{2,1,0:T(8,128)(2,1)}), bf16[32,8,128]{2,1,0:T(8,128)(2,1)S(1)}, u32[]{:S(2)}, u32[]{:S(2)}) %all-to-all-start) | async-done | bytes 65568 | tf_op jit(solution)/shard_map/all_to_all | solution.py:103
  32.3 6.2 %all-to-all-start.2 = ((bf16[32,8,128]{2,1,0:T(8,128)(2,1)}), bf16[32,8,128]{2,1,0:T(8,128)(2,1)S(1)}, u32[]{:S(2)}, u32[]{:S(2)}) async-start(bf16[32,8,128]{2,1,0:T(8,128)(2,1)} %fusion.75), calls=%async_computation.2 | async-start | bytes 131072 | tf_op jit(solution)/shard_map/all_to_all | solution.py:104
  39.3 0.6 fusion.27
  39.8 0.6 fusion.31
  40.4 11.7 %all-to-all-done.2 = bf16[32,8,128]{2,1,0:T(8,128)(2,1)S(1)} async-done(((bf16[32,8,128]{2,1,0:T(8,128)(2,1)}), bf16[32,8,128]{2,1,0:T(8,128)(2,1)S(1)}, u32[]{:S(2)}, u32[]{:S(2)}) %all-to-all-start.2) | async-done | bytes 65568 | tf_op jit(solution)/shard_map/all_to_all | solution.py:104
  52.9 0.6 fusion.15
  53.5 0.6 fusion.19
  54.0 0.6 convolution_subtract_fusion.8
  54.6 0.6 convolution_add_fusion.5
  55.2 0.6 convolution_add_fusion.2
  55.7 0.8 multiply_add_fusion
  56.5 0.5 fusion.82
  57.0 0.5 fusion.98
  58.1 0.5 fusion.106
  58.6 0.5 fusion.85
  59.7 0.5 convolution_add_fusion
  60.2 0.5 convolution_subtract_fusion.1
  60.8 0.9 fusion.36
  61.7 0.9 fusion.5
  62.8 2.8 %fusion = f32[8,1,16]{2,1,0:T(1,128)S(1)} fusion(f32[8,4096,1]{1,2,0:T(1,128)S(1)} %reshape.107, f32[8,16]{1,0:T(8,128)S(1)} %exponential_multiply_fusion), kind=kOutput, calls=%fused_computation | convolution fusion | flops 7864320 | bytes 132096 | tf_op jit(solution)/shard_map/ct,cnt->cn/dot_general | solution.py:120
  65.6 0.5 convolution_add_fusion.3
  66.1 0.7 convolution_subtract_fusion.6
  66.8 0.9 fusion.50
  67.7 0.9 fusion.11
  68.8 0.7 copy.46
  69.4 3.9 %all-to-all-start.1 = ((bf16[8,32,128]{2,0,1:T(8,128)(2,1)}), bf16[8,32,128]{2,0,1:T(8,128)(2,1)S(1)}, u32[]{:S(2)}, u32[]{:S(2)}) async-start(bf16[8,32,128]{2,0,1:T(8,128)(2,1)} %copy.46), calls=%async_computation.1 | async-start | bytes 131072 | tf_op jit(solution)/shard_map/all_to_all | solution.py:114
  73.3 0.5 convolution_add_fusion.1
  73.8 0.5 convolution_subtract_fusion.3
  74.3 0.9 fusion.43
  75.2 0.9 fusion.10
  76.3 0.7 copy.52
  76.9 2.8 %fusion.2 = f32[8,1,16]{2,1,0:T(1,128)S(1)} fusion(f32[8,4096,1]{1,2,0:T(1,128)S(1)} %reshape.107, f32[8,16]{1,0:T(8,128)S(1)} %exponential_multiply_fusion), kind=kOutput, calls=%fused_computation.3 | convolution fusion | flops 7340032 | bytes 132096 | tf_op jit(solution)/shard_map/ct,cnt->cn/dot_general | solution.py:119
  79.8 7.3 %all-to-all-done.1 = bf16[8,32,128]{2,0,1:T(8,128)(2,1)S(1)} async-done(((bf16[8,32,128]{2,0,1:T(8,128)(2,1)}), bf16[8,32,128]{2,0,1:T(8,128)(2,1)S(1)}, u32[]{:S(2)}, u32[]{:S(2)}) %all-to-all-start.1) | async-done | bytes 65568 | tf_op jit(solution)/shard_map/all_to_all | solution.py:114
  87.1 5.8 %all-to-all-start.3 = ((bf16[8,32,128]{2,0,1:T(8,128)(2,1)}), bf16[8,32,128]{2,0,1:T(8,128)(2,1)S(1)}, u32[]{:S(2)}, u32[]{:S(2)}) async-start(bf16[8,32,128]{2,0,1:T(8,128)(2,1)} %copy.52), calls=%async_computation.3 | async-start | bytes 131072 | tf_op jit(solution)/shard_map/all_to_all | solution.py:115
  92.9 63.1 %all_gather.7 = f32[256,16]{1,0:T(8,128)S(1)} all-gather(f32[8,16]{1,0:T(8,128)S(1)} %negate_multiply_fusion), channel_id=1, replica_groups=mesh['ctx'=32,'ch'=16] {'ctx'}, dimensions={0}, use_global_device_ids=true | all-gather | bytes 16896 | tf_op jit(solution)/shard_map/all_gather | solution.py:125
  155.9 0.7 copy.56
  156.6 59.2 %all_gather.6 = f32[256,16]{1,0:T(8,128)S(1)} all-gather(f32[8,16]{1,0:T(8,128)S(1)} %broadcast_multiply_fusion), channel_id=1, replica_groups=mesh['ctx'=32,'ch'=16] {'ctx'}, dimensions={0}, use_global_device_ids=true | all-gather | bytes 16896 | tf_op jit(solution)/shard_map/all_gather | solution.py:124
  215.8 0.7 copy.55
  216.5 0.6 fusion.54
  217.1 0.7 fusion.56
  (42 shorter events, 5.1 us)
Async XLA Ops:
  0.6 18.6 %copy-start.4 = (f32[256,16]{0,1:T(8,128)S(1)}, f32[256,16]{0,1:T(8,128)}, u32[]{:S(2)}) copy-start(f32[256,16]{0,1:T(8,128)} %param.11) | copy-start | bytes 49156
  0.6 18.6 %copy-start.5 = (f32[256,16]{0,1:T(8,128)S(1)}, f32[256,16]{0,1:T(8,128)}, u32[]{:S(2)}) copy-start(f32[256,16]{0,1:T(8,128)} %param.10) | copy-start | bytes 49156
  2.2 30.1 %all-to-all-start = ((bf16[32,8,128]{2,1,0:T(8,128)(2,1)}), bf16[32,8,128]{2,1,0:T(8,128)(2,1)S(1)}, u32[]{:S(2)}, u32[]{:S(2)}) async-start(bf16[32,8,128]{2,1,0:T(8,128)(2,1)} %fusion.74), calls=%async_computation | async-start | bytes 131072 | tf_op jit(solution)/shard_map/all_to_all | solution.py:103
  23.1 0.8 copy-start
  23.1 0.9 copy-start.3
  32.3 19.8 %all-to-all-start.2 = ((bf16[32,8,128]{2,1,0:T(8,128)(2,1)}), bf16[32,8,128]{2,1,0:T(8,128)(2,1)S(1)}, u32[]{:S(2)}, u32[]{:S(2)}) async-start(bf16[32,8,128]{2,1,0:T(8,128)(2,1)} %fusion.75), calls=%async_computation.2 | async-start | bytes 131072 | tf_op jit(solution)/shard_map/all_to_all | solution.py:104
  69.4 17.6 %all-to-all-start.1 = ((bf16[8,32,128]{2,0,1:T(8,128)(2,1)}), bf16[8,32,128]{2,0,1:T(8,128)(2,1)S(1)}, u32[]{:S(2)}, u32[]{:S(2)}) async-start(bf16[8,32,128]{2,0,1:T(8,128)(2,1)} %copy.46), calls=%async_computation.1 | async-start | bytes 131072 | tf_op jit(solution)/shard_map/all_to_all | solution.py:114
  87.1 130.0 %all-to-all-start.3 = ((bf16[8,32,128]{2,0,1:T(8,128)(2,1)}), bf16[8,32,128]{2,0,1:T(8,128)(2,1)S(1)}, u32[]{:S(2)}, u32[]{:S(2)}) async-start(bf16[8,32,128]{2,0,1:T(8,128)(2,1)} %copy.52), calls=%async_computation.3 | async-start | bytes 131072 | tf_op jit(solution)/shard_map/all_to_all | solution.py:115
  156.6 60.5 %copy-start.1 = (bf16[256,128]{1,0:T(8,128)(2,1)S(1)}, bf16[256,128]{1,0:T(8,128)(2,1)}, u32[]{:S(2)}) copy-start(bf16[256,128]{1,0:T(8,128)(2,1)} %param.8) | copy-start | bytes 196612
  156.6 60.5 %copy-start.2 = (bf16[256,128]{1,0:T(8,128)(2,1)S(1)}, bf16[256,128]{1,0:T(8,128)(2,1)}, u32[]{:S(2)}) copy-start(bf16[256,128]{1,0:T(8,128)(2,1)} %param.7) | copy-start | bytes 196612
where the time goes:
time: 219 us; the launch traced here: 218 us
  blocking collectives  122 us (56%)
  starting transfers between devices  32.2 us (15%)
  matrix products  27.6 us (13%)
  waiting for transfers between devices  26.1 us (12%)
  local copies, waits for them, and re-layouts  4.31 us (2%)
  other arithmetic  4.27 us (2%)
    all_gather x1, blocking collectives, exchange_plan(): lax.all_gather(grad_log, 'ctx', axis=0, tiled=True)  63.1 us
    all_gather x1, blocking collectives, exchange_plan(): lax.all_gather(grad_res, 'ctx', axis=0, tiled=True)  59.2 us
    all_to_all x1, starting transfers between devices, exchange_plan(): lax.all_to_all(mixed_input, 'ctx', split_axis=0, concat_axis=1, tiled=True)  16.4 us
    all_to_all x1, waiting for transfers between devices, exchange_plan(): lax.all_to_all(grad_conv, 'ctx', split_axis=0, concat_axis=1, tiled=True)  11.7 us
    all_to_all x1, waiting for transfers between devices, exchange_plan(): lax.all_to_all(conv_seq, 'ctx', split_axis=1, concat_axis=0, tiled=True)  7.3 us
    all_to_all x1, waiting for transfers between devices, exchange_plan(): lax.all_to_all(mixed_input, 'ctx', split_axis=0, concat_axis=1, tiled=True)  7.09 us
    all_to_all x1, starting transfers between devices, exchange_plan(): lax.all_to_all(grad_conv, 'ctx', split_axis=0, concat_axis=1, tiled=True)  6.18 us
    all_to_all x1, starting transfers between devices, exchange_plan(): lax.all_to_all(input_seq, 'ctx', split_axis=1, concat_axis=0, tiled=True)  5.8 us
  transfers between devices with their start and end apart: 4, of which 3 were waited for; matrix products, arithmetic and copies ran while one was open for 8% of the time, Pallas kernels for 0%

commit v1 on v0

v1 whole, which is shorter than its diff:
```python
import functools

import jax
import jax.numpy as jnp
from jax import lax
from jax.experimental import pallas as pl
from jax.experimental.pallas import tpu as pltpu
from jax.sharding import PartitionSpec as P

F32 = jnp.float32
BF16 = jnp.bfloat16
POLES = 16
BLOCK = 8
LANES = 128


def gated(left_ref, right_ref):
    product = (left_ref[...].astype(F32) * right_ref[...].astype(F32)).astype(BF16)
    return product.astype(F32).T


def pole_rows(residue_ref, log_ref):
    channels = residue_ref.shape[0]
    filler = jnp.zeros((channels, LANES - 2 * POLES), F32)
    both = jnp.concatenate([residue_ref[...], log_ref[...], filler], axis=1).T
    return both[:POLES], both[POLES : 2 * POLES]


def summary_kernel(length, key_ref, value_ref, query_ref, out_grad_ref, residue_ref, log_ref, out_ref, mixed, grad):
    width, channels = mixed.shape
    mixed[...] = gated(key_ref, value_ref)
    grad[...] = gated(query_ref, out_grad_ref)
    _, log_rows = pole_rows(residue_ref, log_ref)
    decay = jnp.exp(-(jnp.exp(log_rows) / length))
    zero = jnp.zeros((POLES, channels), F32)

    def step(block, carry):
        state, moment, res, rate, back, back_moment = carry
        first = block * BLOCK
        for row in range(BLOCK):
            mixed_row = mixed[pl.ds(first + row, 1), :]
            grad_row = grad[pl.ds(first + row, 1), :]
            late_row = grad[pl.ds(width - 1 - first - row, 1), :]
            faded = decay * state
            state = faded + mixed_row
            moment = decay * moment + faded
            res = res + grad_row * state
            rate = rate + grad_row * moment
            faded = decay * back
            back = faded + late_row
            back_moment = decay * back_moment + faded
        return state, moment, res, rate, back, back_moment

    state, moment, res, rate, back, back_moment = lax.fori_loop(0, width // BLOCK, step, (zero,) * 6)
    last = decay * state
    last_moment = decay * moment + last
    rows = [last, back, last_moment, back_moment, res, rate, zero, zero]
    out_ref[...] = jnp.concatenate(rows, axis=0).T.reshape(out_ref.shape)


def local_kernel(
    length,
    place_ref,
    key_ref,
    value_ref,
    query_ref,
    out_grad_ref,
    residue_ref,
    log_ref,
    conv_ref,
    back_ref,
    ahead_ref,
    behind_ref,
    fade_ref,
    chunk_ref,
    mixed,
    grad,
):
    width, channels = mixed.shape
    mixed[...] = gated(key_ref, value_ref)
    grad[...] = gated(query_ref, out_grad_ref)
    residue_rows, log_rows = pole_rows(residue_ref, log_ref)
    rates = jnp.exp(log_rows) / length
    decay = jnp.exp(-rates)
    weight = residue_rows * (length**-0.5)
    zero = jnp.zeros((POLES, channels), F32)

    def step(block, carry):
        state, back = carry
        first = pl.multiple_of(block * BLOCK, BLOCK)
        last = pl.multiple_of(width - BLOCK - block * BLOCK, BLOCK)
        ahead, behind = [], []
        for row in range(BLOCK):
            state = decay * state + mixed[pl.ds(first + row, 1), :]
            ahead.append(jnp.sum(weight * state, axis=0, keepdims=True))
            back = decay * back + grad[pl.ds(last + BLOCK - 1 - row, 1), :]
            behind.append(jnp.sum(weight * back, axis=0, keepdims=True))
        conv_ref[pl.ds(first, BLOCK), :] = jnp.concatenate(ahead, axis=0)
        back_ref[pl.ds(last, BLOCK), :] = jnp.concatenate(behind[::-1], axis=0)
        return state, back

    lax.fori_loop(0, width // BLOCK, step, (zero, zero))
    steps = lax.broadcasted_iota(jnp.int32, (BLOCK, channels), 0).astype(F32)
    for pole in range(POLES):
        rate = rates[pole : pole + 1]
        scale = weight[pole : pole + 1]
        ahead_ref[pole] = scale * jnp.exp(-(rate * steps))
        behind_ref[pole] = scale * jnp.exp(-(rate * (BLOCK - steps)))
    fade_ref[...] = jnp.exp(-(rates * BLOCK))
    own = log_ref[pl.ds(pl.multiple_of(place_ref[0] * BLOCK, BLOCK), BLOCK), :]
    own_rates = jnp.exp(jnp.concatenate([own] * (LANES // POLES), axis=1)) / length
    chunk_ref[...] = jnp.exp(-(own_rates * width))


def prefix_kernel(width, parts_ref, chunk_ref, out_ref):
    chunks = parts_ref.shape[0]
    fade = chunk_ref[...]
    lane = lax.broadcasted_iota(jnp.int32, fade.shape, 1)
    zero = jnp.zeros(fade.shape, F32)

    def shifted(part, places):
        return pltpu.roll(part, LANES - places * POLES, 1)

    parts = [parts_ref[chunk] for chunk in range(chunks)]
    state, moment, res, rate = zero, zero, zero, zero
    states = []
    for part in parts:
        states.append(state)
        back = shifted(part, 1)
        res = res + back * state
        rate = rate + shifted(part, 3) * state + back * moment
        moment = fade * (moment + width * state) + shifted(part, 2)
        state = fade * state + part
    local = functools.reduce(lambda a, b: a + b, parts)
    totals = pltpu.roll(res, 2 * POLES, 1)
    totals = jnp.where(lane < 3 * POLES, totals, pltpu.roll(rate, 3 * POLES, 1))
    totals = totals + pltpu.roll(local, LANES - 2 * POLES, 1)
    back = zero
    for chunk in range(chunks - 1, -1, -1):
        sent = jnp.where(lane < POLES, states[chunk], jnp.where(lane < 2 * POLES, back, totals))
        out_ref[chunk] = sent
        back = fade * back + parts[chunk]


def output_kernel(
    length,
    carried_ref,
    conv_ref,
    back_ref,
    ahead_ref,
    behind_ref,
    fade_ref,
    key_ref,
    value_ref,
    out_grad_ref,
    residue_ref,
    log_ref,
    query_out,
    key_out,
    value_out,
    residue_out,
    log_out,
):
    channels = residue_ref.shape[0]
    width = conv_ref.shape[0]
    blocks = width // BLOCK
    carried = carried_ref[...].reshape(channels, LANES)
    rows = carried.T
    residue_out[...] = carried[:, 2 * POLES : 3 * POLES] * (1.0 / length)
    rates = jnp.exp(log_ref[...]) / length
    log_out[...] = -(residue_ref[...] / length) * rates * carried[:, 3 * POLES : 4 * POLES]
    for half in range(channels // LANES):
        here = slice(half * LANES, (half + 1) * LANES)
        total = [conv_ref[block * BLOCK : (block + 1) * BLOCK, here] for block in range(blocks)]
        for pole in range(POLES):
            term = ahead_ref[pole, :, here] * rows[pole : pole + 1, here]
            fade = fade_ref[pole : pole + 1, here]
            for block in range(blocks):
                total[block] = total[block] + term
                term = term * fade
        conv = jnp.concatenate(total, axis=0).T.astype(BF16).astype(F32)
        query_out[here, :] = (out_grad_ref[here, :].astype(F32) * conv).astype(BF16)
        total = [back_ref[block * BLOCK : (block + 1) * BLOCK, here] for block in range(blocks)]
        for pole in range(POLES):
            term = behind_ref[pole, :, here] * rows[POLES + pole : POLES + pole + 1, here]
            fade = fade_ref[pole : pole + 1, here]
            for block in range(blocks - 1, -1, -1):
                total[block] = total[block] + term
                term = term * fade
        back = jnp.concatenate(total, axis=0).T.astype(BF16).astype(F32)
        key_out[here, :] = (back * value_ref[here, :].astype(F32)).astype(BF16)
        value_out[here, :] = (back * key_ref[here, :].astype(F32)).astype(BF16)


def on_device(query, key_gate, value_in, grad_output, residue, log_rate):
    chunks = lax.axis_size("ctx")
    channels, width = query.shape
    length = width * chunks
    struct = jax.ShapeDtypeStruct
    in_vmem = pl.BlockSpec(memory_space=pltpu.VMEM)
    turned = [pltpu.VMEM((width, channels), F32)] * 2
    params = pltpu.CompilerParams(vmem_limit_bytes=32 * 1024 * 1024)
    gates = (key_gate, value_in, query, grad_output, residue, log_rate)
    sent = struct((chunks, channels // chunks, LANES), F32)

    summary = pl.pallas_call(
        functools.partial(summary_kernel, float(length)),
        out_shape=sent,
        in_specs=[in_vmem] * 6,
        out_specs=in_vmem,
        scratch_shapes=turned,
        compiler_params=params,
        name="chunk_summary",
    )(*gates)
    parts = lax.all_to_all(summary, "ctx", split_axis=0, concat_axis=0, tiled=True)
    place = lax.axis_index("ctx").astype(jnp.int32).reshape(1)
    conv, back, ahead, behind, fade, chunk_fade = pl.pallas_call(
        functools.partial(local_kernel, float(length)),
        out_shape=(
            struct((width, channels), F32),
            struct((width, channels), F32),
            struct((POLES, BLOCK, channels), F32),
            struct((POLES, BLOCK, channels), F32),
            struct((POLES, channels), F32),
            struct((BLOCK, LANES), F32),
        ),
        in_specs=[pl.BlockSpec(memory_space=pltpu.SMEM)] + [in_vmem] * 6,
        out_specs=[in_vmem] * 6,
        scratch_shapes=turned,
        compiler_params=params,
        name="local_part",
        cost_estimate=pl.CostEstimate(flops=20_000_000, bytes_accessed=1_500_000, transcendentals=0),
    )(place, *gates)
    carried = pl.pallas_call(
        functools.partial(prefix_kernel, float(width)),
        out_shape=sent,
        in_specs=[in_vmem] * 2,
        out_specs=in_vmem,
        compiler_params=params,
        name="chunk_prefix",
    )(parts, chunk_fade)
    carried = lax.all_to_all(carried, "ctx", split_axis=0, concat_axis=0, tiled=True)
    gate_out = struct((channels, width), BF16)
    pole_out = struct((channels, POLES), F32)
    return pl.pallas_call(
        functools.partial(output_kernel, float(length)),
        out_shape=(gate_out, gate_out, gate_out, pole_out, pole_out),
        in_specs=[in_vmem] * 11,
        out_specs=[in_vmem] * 5,
        compiler_params=params,
        name="outputs",
    )(carried, conv, back, ahead, behind, fade, key_gate, value_in, grad_output, residue, log_rate)


def solution(mesh):
    both = P("ch", "ctx")
    rows = P("ch", None)
    return jax.shard_map(
        on_device,
        mesh=mesh,
        in_specs=(both, both, both, both, rows, rows),
        out_specs=(both, both, both, rows, rows),
        check_vma=False,
    )
```

time: 219 us -> 59 us (0.27)
  blocking collectives: 122 us -> 18.9 us
  matrix products: 27.6 us -> 0 us
  starting transfers between devices: 32.2 us -> 16.4 us
  waiting for transfers between devices: 26.1 us -> 15 us
  Pallas kernels: 0 us -> 4.54 us
  other arithmetic: 4.27 us -> 0 us
    all_gather x2 -> x0, blocking collectives: 122 us -> none  [the longest x1 63.1 us: exchange_plan(): lax.all_gather(grad_log, 'ctx', axis=0, tiled=True)]
    dot_general x33 -> x0, matrix products: 25.9 us -> none  [the longest x1 2.83 us: exchange_plan(): jnp.einsum('ct,cnt->cn', filt_grad, decay_table, precision=PRECISE) / length]
    all_to_all x0 -> x1, blocking collectives: none -> 18.9 us  [on_device(): lax.all_to_all(carried, 'ctx', split_axis=0, concat_axis=0, tiled=True)]
    all_to_all x4 -> x1, starting transfers between devices: 32.2 us -> 16.4 us  [on_device(): lax.all_to_all(summary, 'ctx', split_axis=0, concat_axis=0, tiled=True)]
    all_to_all x4 -> x1, waiting for transfers between devices: 26.1 us -> 15 us  [on_device(): lax.all_to_all(summary, 'ctx', split_axis=0, concat_axis=0, tiled=True)]
    pallas_call x0 -> x4, Pallas kernels: none -> 4.54 us  [the longest x1 1.84 us: on_device(): pl.pallas_call(functools.partial(summary_kernel, float(length)), out_shap...]
  transfers between devices with their start and end apart: 4 -> 1, of which waited for: 3 -> 1; matrix products, arithmetic and copies ran while one was open for 8% -> 0% of each run, Pallas kernels for 0% -> 2%
where the time goes in v1:
time: 59 us; the launch traced here: 58.7 us
  blocking collectives  18.9 us (32%)
  starting transfers between devices  16.4 us (28%)
  waiting for transfers between devices  15 us (25%)
  Pallas kernels  4.54 us (8%)
  local copies, waits for them, and re-layouts  3.06 us (5%)
  between operations  0.72 us (1%)
    all_to_all x1, blocking collectives, on_device(): lax.all_to_all(carried, 'ctx', split_axis=0, concat_axis=0, tiled=True)  18.9 us
    all_to_all x1, starting transfers between devices, on_device(): lax.all_to_all(summary, 'ctx', split_axis=0, concat_axis=0, tiled=True)  16.4 us
    all_to_all x1, waiting for transfers between devices, on_device(): lax.all_to_all(summary, 'ctx', split_axis=0, concat_axis=0, tiled=True)  15 us
    pallas_call x1, Pallas kernels, on_device(): pl.pallas_call(functools.partial(summary_kernel, float(length)), out_shap...  1.84 us
    unnamed x12, local copies, waits for them, and re-layouts  1.71 us
    pallas_call x2, local copies, waits for them, and re-layouts, on_device(): pl.pallas_call(functools.partial(output_kernel, float(length)), out_shape...  1.35 us
    pallas_call x1, Pallas kernels, on_device(): pl.pallas_call(functools.partial(local_kernel, float(length)), out_shape=...  1.29 us
  transfers between devices with their start and end apart: 1, of which 1 were waited for; matrix products, arithmetic and copies ran while one was open for 0% of the time, Pallas kernels for 2%

profile of v1, /device:TPU:24, one launch (start us, length us, event | category | flops | bytes accessed | tf_op | source)
XLA Modules:
  0.0 58.7 jit_solution(5678299738917679551)
XLA Ops:
  0.6 0.0 copy-start.4
  0.6 0.0 copy-start.2
  0.7 0.0 copy-start.3
  0.7 0.9 %copy.11.residue_ref = f32[256,16]{1,0:T(8,128)S(1)} copy(f32[256,16]{0,1:T(8,128)} %param.10) | data formatting | bytes 32768 | tf_op args[4]
  1.5 0.0 copy-done.4
  1.5 0.0 copy-start
  1.5 0.0 copy-start.1
  1.5 0.1 copy.12.log_ref
  1.6 0.0 copy-done.2
  1.6 0.0 copy-done.3
  1.7 0.7 %copy-done = bf16[256,128]{1,0:T(8,128)(2,1)S(1)} copy-done((bf16[256,128]{1,0:T(8,128)(2,1)S(1)}, bf16[256,128]{1,0:T(8,128)(2,1)}, u32[]{:S(2)}) %copy-start) | copy-done | bytes 65560
  2.4 0.0 copy-done.1
  2.4 1.8 %chunk_summary.1 = f32[32,8,128]{2,1,0:T(8,128)} custom-call(bf16[256,128]{1,0:T(8,128)(2,1)S(1)} %copy-done, bf16[256,128]{1,0:T(8,128)(2,1)S(1)} %copy-done.1, bf16[256,128]{1,0:T(8,128)(2,1)S(1)} %copy-done.3, bf16[256,128]{1,0:T(8,128)(2,1)S(1)} %copy-done.2, f32[256,16]{1,0:T(8,128)S(1)} %copy.11.residue_ref, f32[256,16]{1,0:T(8,128)S(1)} %copy.12.log_ref), custom_call_target="tpu_custom_call" | custom-call | tf_op jit(solution)/shard_map/chunk_summary/pallas_call | solution.py:206
  4.2 16.4 %all-to-all-start = ((f32[32,8,128]{2,1,0:T(8,128)}), f32[32,8,128]{2,1,0:T(8,128)S(1)}, u32[]{:S(2)}, u32[]{:S(2)}) async-start(f32[32,8,128]{2,1,0:T(8,128)} %chunk_summary.1), calls=%async_computation | async-start | bytes 262144 | tf_op jit(solution)/shard_map/all_to_all | solution.py:215
  20.7 1.3 %local_part.1 = (f32[128,256]{1,0:T(8,128)S(1)}, f32[128,256]{1,0:T(8,128)S(1)}, f32[16,8,256]{2,1,0:T(8,128)S(1)}, f32[16,8,256]{2,1,0:T(8,128)S(1)}, f32[16,256]{1,0:T(8,128)S(1)}, /*index=5*/f32[8,128]{1,0:T(8,128)S(1)}) custom-call(s32[1]{0:T(128)} %bitcast.place_ref, bf16[256,128]{1,0:T(8,128)(2,1)S(1)} %copy-done, bf16[256,128]{1,0:T(8,128)(2,1)S(1)} %copy-done.1, ...), custom_call_target="tpu_custom_call" | custom-call | flops 20000000 | bytes 1500000 | tf_op jit(solution)/shard_map/local_part/pallas_call | solution.py:217
  21.9 15.0 %all-to-all-done.parts_ref = f32[32,8,128]{2,1,0:T(8,128)S(1)} async-done(((f32[32,8,128]{2,1,0:T(8,128)}), f32[32,8,128]{2,1,0:T(8,128)S(1)}, u32[]{:S(2)}, u32[]{:S(2)}) %all-to-all-start) | async-done | bytes 131104 | tf_op jit(solution)/shard_map/all_to_all | solution.py:215
  37.0 0.2 chunk_prefix.1
  37.3 18.9 %all_to_all.10.carried_ref = f32[32,8,128]{2,1,0:T(8,128)S(1)} all-to-all(f32[32,8,128]{2,1,0:T(8,128)S(1)} %chunk_prefix.1), channel_id=1, replica_groups=mesh['ctx'=32,'ch'=16] {'ctx'}, dimensions={0} | all-to-all | bytes 262144 | tf_op jit(solution)/shard_map/all_to_all | solution.py:242
  56.2 1.2 %outputs.1 = (bf16[256,128]{1,0:T(8,128)(2,1)}, bf16[256,128]{1,0:T(8,128)(2,1)}, bf16[256,128]{1,0:T(8,128)(2,1)}, f32[256,16]{1,0:T(8,128)S(1)}, f32[256,16]{1,0:T(8,128)S(1)}) custom-call(f32[32,8,128]{2,1,0:T(8,128)S(1)} %all_to_all.10.carried_ref, f32[128,256]{1,0:T(8,128)S(1)} %get-tuple-element.12.conv_ref, ...), custom_call_target="tpu_custom_call" | custom-call | tf_op jit(solution)/shard_map/outputs/pallas_call | solution.py:245
  57.4 0.7 %copy.17 = f32[256,16]{0,1:T(8,128)} copy(f32[256,16]{1,0:T(8,128)S(1)} %get-tuple-element.20) | data formatting | bytes 32768 | tf_op jit(solution)/shard_map/outputs/pallas_call | solution.py:245
  58.0 0.7 %copy.18 = f32[256,16]{0,1:T(8,128)} copy(f32[256,16]{1,0:T(8,128)S(1)} %get-tuple-element.21) | data formatting | bytes 32768 | tf_op jit(solution)/shard_map/outputs/pallas_call | solution.py:245
Async XLA Ops:
  0.6 0.9 %copy-start.4 = (f32[256,16]{0,1:T(8,128)S(1)}, f32[256,16]{0,1:T(8,128)}, u32[]{:S(2)}) copy-start(f32[256,16]{0,1:T(8,128)} %param.11) | copy-start | bytes 49156
  0.6 1.0 %copy-start.2 = (bf16[256,128]{1,0:T(8,128)(2,1)S(1)}, bf16[256,128]{1,0:T(8,128)(2,1)}, u32[]{:S(2)}) copy-start(bf16[256,128]{1,0:T(8,128)(2,1)} %out_grad_ref.5) | copy-start | bytes 196612
  0.7 1.0 %copy-start.3 = (bf16[256,128]{1,0:T(8,128)(2,1)S(1)}, bf16[256,128]{1,0:T(8,128)(2,1)}, u32[]{:S(2)}) copy-start(bf16[256,128]{1,0:T(8,128)(2,1)} %query_ref.3) | copy-start | bytes 196612
  1.5 0.8 %copy-start = (bf16[256,128]{1,0:T(8,128)(2,1)S(1)}, bf16[256,128]{1,0:T(8,128)(2,1)}, u32[]{:S(2)}) copy-start(bf16[256,128]{1,0:T(8,128)(2,1)} %key_ref.5) | copy-start | bytes 196612
  1.5 0.9 %copy-start.1 = (bf16[256,128]{1,0:T(8,128)(2,1)S(1)}, bf16[256,128]{1,0:T(8,128)(2,1)}, u32[]{:S(2)}) copy-start(bf16[256,128]{1,0:T(8,128)(2,1)} %value_ref.5) | copy-start | bytes 196612
  4.2 32.8 %all-to-all-start = ((f32[32,8,128]{2,1,0:T(8,128)}), f32[32,8,128]{2,1,0:T(8,128)S(1)}, u32[]{:S(2)}, u32[]{:S(2)}) async-start(f32[32,8,128]{2,1,0:T(8,128)} %chunk_summary.1), calls=%async_computation | async-start | bytes 262144 | tf_op jit(solution)/shard_map/all_to_all | solution.py:215

commit v2 on v1

--- a/solution.py
+++ b/solution.py
@@ -19,19 +19,15 @@
     return product.astype(F32).T
 
 
-def pole_rows(residue_ref, log_ref):
-    channels = residue_ref.shape[0]
-    filler = jnp.zeros((channels, LANES - 2 * POLES), F32)
-    both = jnp.concatenate([residue_ref[...], log_ref[...], filler], axis=1).T
-    return both[:POLES], both[POLES : 2 * POLES]
-
-
-def summary_kernel(length, key_ref, value_ref, query_ref, out_grad_ref, residue_ref, log_ref, out_ref, mixed, grad):
+def rounded(value):
+    return value.astype(BF16).astype(F32)
+
+
+def summary_kernel(length, key_ref, value_ref, query_ref, out_grad_ref, log_ref, out_ref, mixed, grad):
     width, channels = mixed.shape
     mixed[...] = gated(key_ref, value_ref)
     grad[...] = gated(query_ref, out_grad_ref)
-    _, log_rows = pole_rows(residue_ref, log_ref)
-    decay = jnp.exp(-(jnp.exp(log_rows) / length))
+    decay = jnp.exp(-(jnp.exp(log_ref[...]) / length))
     zero = jnp.zeros((POLES, channels), F32)
 
     def step(block, carry):
@@ -54,8 +50,9 @@
     state, moment, res, rate, back, back_moment = lax.fori_loop(0, width // BLOCK, step, (zero,) * 6)
     last = decay * state
     last_moment = decay * moment + last
-    rows = [last, back, last_moment, back_moment, res, rate, zero, zero]
-    out_ref[...] = jnp.concatenate(rows, axis=0).T.reshape(out_ref.shape)
+    rest = [last - rounded(last), back - rounded(back)]
+    rows = [last, back, last_moment, back_moment, res, rate] + rest
+    out_ref[...] = jnp.concatenate(rows, axis=0).T.astype(BF16)
 
 
 def local_kernel(
@@ -75,14 +72,14 @@
     chunk_ref,
     mixed,
     grad,
+    logs,
 ):
     width, channels = mixed.shape
     mixed[...] = gated(key_ref, value_ref)
     grad[...] = gated(query_ref, out_grad_ref)
-    residue_rows, log_rows = pole_rows(residue_ref, log_ref)
-    rates = jnp.exp(log_rows) / length
+    rates = jnp.exp(log_ref[...]) / length
     decay = jnp.exp(-rates)
-    weight = residue_rows * (length**-0.5)
+    weight = residue_ref[...] * (length**-0.5)
     zero = jnp.zeros((POLES, channels), F32)
 
     def step(block, carry):
@@ -107,13 +104,13 @@
         ahead_ref[pole] = scale * jnp.exp(-(rate * steps))
         behind_ref[pole] = scale * jnp.exp(-(rate * (BLOCK - steps)))
     fade_ref[...] = jnp.exp(-(rates * BLOCK))
-    own = log_ref[pl.ds(pl.multiple_of(place_ref[0] * BLOCK, BLOCK), BLOCK), :]
-    own_rates = jnp.exp(jnp.concatenate([own] * (LANES // POLES), axis=1)) / length
-    chunk_ref[...] = jnp.exp(-(own_rates * width))
+    logs[...] = jnp.concatenate([log_ref[...]] * (LANES // POLES), axis=0).T
+    own = logs[pl.ds(pl.multiple_of(place_ref[0] * BLOCK, BLOCK), BLOCK), :]
+    chunk_ref[...] = jnp.exp(-(jnp.exp(own) / length * width))
 
 
 def prefix_kernel(width, parts_ref, chunk_ref, out_ref):
-    chunks = parts_ref.shape[0]
+    chunks = parts_ref.shape[0] // BLOCK
     fade = chunk_ref[...]
     lane = lax.broadcasted_iota(jnp.int32, fade.shape, 1)
     zero = jnp.zeros(fade.shape, F32)
@@ -121,25 +118,33 @@
     def shifted(part, places):
         return pltpu.roll(part, LANES - places * POLES, 1)
 
-    parts = [parts_ref[chunk] for chunk in range(chunks)]
+    parts = []
+    for pair in range(chunks // 2):
+        both = parts_ref[pair * 2 * BLOCK : (pair + 1) * 2 * BLOCK, :].astype(F32)
+        parts += [both[:BLOCK], both[BLOCK:]]
+    ends = [part + shifted(part, 6) for part in parts]
     state, moment, res, rate = zero, zero, zero, zero
     states = []
-    for part in parts:
+    for part, end in zip(parts, ends):
         states.append(state)
-        back = shifted(part, 1)
+        back = shifted(end, 1)
         res = res + back * state
         rate = rate + shifted(part, 3) * state + back * moment
         moment = fade * (moment + width * state) + shifted(part, 2)
-        state = fade * state + part
+        state = fade * state + end
     local = functools.reduce(lambda a, b: a + b, parts)
-    totals = pltpu.roll(res, 2 * POLES, 1)
-    totals = jnp.where(lane < 3 * POLES, totals, pltpu.roll(rate, 3 * POLES, 1))
-    totals = totals + pltpu.roll(local, LANES - 2 * POLES, 1)
+    totals = jnp.where(lane < 3 * POLES, pltpu.roll(res, 2 * POLES, 1), pltpu.roll(rate, 3 * POLES, 1))
+    totals = totals + shifted(local, 2)
     back = zero
+    sent = [None] * chunks
     for chunk in range(chunks - 1, -1, -1):
-        sent = jnp.where(lane < POLES, states[chunk], jnp.where(lane < 2 * POLES, back, totals))
-        out_ref[chunk] = sent
-        back = fade * back + parts[chunk]
+        whole = jnp.where(lane < POLES, states[chunk], jnp.where(lane < 2 * POLES, back, totals))
+        rest = pltpu.roll(whole - rounded(whole), LANES // 2, 1)
+        sent[chunk] = jnp.where(lane < LANES // 2, whole, rest)
+        back = fade * back + ends[chunk]
+    for pair in range(chunks // 2):
+        both = jnp.concatenate(sent[2 * pair : 2 * pair + 2], axis=0)
+        out_ref[pair * 2 * BLOCK : (pair + 1) * 2 * BLOCK, :] = both.astype(BF16)
 
 
 def output_kernel(
@@ -161,14 +166,13 @@
     residue_out,
     log_out,
 ):
-    channels = residue_ref.shape[0]
-    width = conv_ref.shape[0]
+    width, channels = conv_ref.shape
     blocks = width // BLOCK
-    carried = carried_ref[...].reshape(channels, LANES)
-    rows = carried.T
-    residue_out[...] = carried[:, 2 * POLES : 3 * POLES] * (1.0 / length)
+    rows = carried_ref[...].astype(F32).T
+    rows = rows[: LANES // 2] + rows[LANES // 2 :]
+    residue_out[...] = rows[2 * POLES : 3 * POLES] * (1.0 / length)
     rates = jnp.exp(log_ref[...]) / length
-    log_out[...] = -(residue_ref[...] / length) * rates * carried[:, 3 * POLES : 4 * POLES]
+    log_out[...] = -(residue_ref[...] / length) * rates * rows[3 * POLES :]
     for half in range(channels // LANES):
         here = slice(half * LANES, (half + 1) * LANES)
         total = [conv_ref[block * BLOCK : (block + 1) * BLOCK, here] for block in range(blocks)]
@@ -200,19 +204,25 @@
     in_vmem = pl.BlockSpec(memory_space=pltpu.VMEM)
     turned = [pltpu.VMEM((width, channels), F32)] * 2
     params = pltpu.CompilerParams(vmem_limit_bytes=32 * 1024 * 1024)
-    gates = (key_gate, value_in, query, grad_output, residue, log_rate)
-    sent = struct((chunks, channels // chunks, LANES), F32)
+    gates = (key_gate, value_in, query, grad_output)
+    poles = (residue.T, log_rate.T)
+    sent = struct((channels, LANES), BF16)
+    per_chunk = (chunks, channels // chunks, LANES)
+
+    def exchange(table):
+        table = lax.all_to_all(table.reshape(per_chunk), "ctx", split_axis=0, concat_axis=0, tiled=True)
+        return table.reshape(channels, LANES)
 
     summary = pl.pallas_call(
         functools.partial(summary_kernel, float(length)),
         out_shape=sent,
-        in_specs=[in_vmem] * 6,
+        in_specs=[in_vmem] * 5,
         out_specs=in_vmem,
         scratch_shapes=turned,
         compiler_params=params,
         name="chunk_summary",
-    )(*gates)
-    parts = lax.all_to_all(summary, "ctx", split_axis=0, concat_axis=0, tiled=True)
+    )(*gates, poles[1])
+    parts = exchange(summary)
     place = lax.axis_index("ctx").astype(jnp.int32).reshape(1)
     conv, back, ahead, behind, fade, chunk_fade = pl.pallas_call(
         functools.partial(local_kernel, float(length)),
@@ -226,11 +236,11 @@
         ),
         in_specs=[pl.BlockSpec(memory_space=pltpu.SMEM)] + [in_vmem] * 6,
         out_specs=[in_vmem] * 6,
-        scratch_shapes=turned,
+        scratch_shapes=turned + [pltpu.VMEM((channels, LANES), F32)],
         compiler_params=params,
         name="local_part",
         cost_estimate=pl.CostEstimate(flops=20_000_000, bytes_accessed=1_500_000, transcendentals=0),
-    )(place, *gates)
+    )(place, *gates, *poles)
     carried = pl.pallas_call(
         functools.partial(prefix_kernel, float(width)),
         out_shape=sent,
@@ -239,17 +249,18 @@
         compiler_params=params,
         name="chunk_prefix",
     )(parts, chunk_fade)
-    carried = lax.all_to_all(carried, "ctx", split_axis=0, concat_axis=0, tiled=True)
+    carried = exchange(carried)
     gate_out = struct((channels, width), BF16)
-    pole_out = struct((channels, POLES), F32)
-    return pl.pallas_call(
+    pole_out = struct((POLES, channels), F32)
+    outs = pl.pallas_call(
         functools.partial(output_kernel, float(length)),
         out_shape=(gate_out, gate_out, gate_out, pole_out, pole_out),
         in_specs=[in_vmem] * 11,
         out_specs=[in_vmem] * 5,
         compiler_params=params,
         name="outputs",
-    )(carried, conv, back, ahead, behind, fade, key_gate, value_in, grad_output, residue, log_rate)
+    )(carried, conv, back, ahead, behind, fade, key_gate, value_in, grad_output, *poles)
+    return (*outs[:3], outs[3].T, outs[4].T)
 
 
 def solution(mesh):

time: 59 us -> 55.5 us (0.941)
  waiting for transfers between devices: 15 us -> 12.4 us
  blocking collectives: 18.9 us -> 16.7 us
  local copies, waits for them, and re-layouts: 3.06 us -> 4.09 us
    all_to_all x1, waiting for transfers between devices: 15 us -> 12.4 us  [exchange(): lax.all_to_all(table.reshape(per_chunk), 'ctx', split_axis=0, concat_axis...]
    unnamed x12 -> x22, local copies, waits for them, and re-layouts: 1.71 us -> 4.09 us
    all_to_all x1, blocking collectives: 18.9 us -> 16.7 us  [exchange(): lax.all_to_all(table.reshape(per_chunk), 'ctx', split_axis=0, concat_axis...]
    pallas_call x2 -> x0, local copies, waits for them, and re-layouts: 1.35 us -> none  [on_device(): pl.pallas_call(functools.partial(output_kernel, float(length)), out_shape...]
where the time goes in v2:
time: 55.5 us; the launch traced here: 55 us
  blocking collectives  16.7 us (30%)
  starting transfers between devices  16.5 us (30%)
  waiting for transfers between devices  12.4 us (22%)
  Pallas kernels  4.61 us (8%)
  local copies, waits for them, and re-layouts  4.09 us (7%)
  between operations  0.72 us (1%)
    all_to_all x1, blocking collectives, exchange(): lax.all_to_all(table.reshape(per_chunk), 'ctx', split_axis=0, concat_axis...  16.7 us
    all_to_all x1, starting transfers between devices, exchange(): lax.all_to_all(table.reshape(per_chunk), 'ctx', split_axis=0, concat_axis...  16.5 us
    all_to_all x1, waiting for transfers between devices, exchange(): lax.all_to_all(table.reshape(per_chunk), 'ctx', split_axis=0, concat_axis...  12.4 us
    unnamed x22, local copies, waits for them, and re-layouts  4.09 us
    pallas_call x1, Pallas kernels, on_device(): pl.pallas_call(functools.partial(summary_kernel, float(length)), out_shap...  1.77 us
    pallas_call x1, Pallas kernels, on_device(): pl.pallas_call(functools.partial(local_kernel, float(length)), out_shape=...  1.24 us
    pallas_call x1, Pallas kernels, on_device(): pl.pallas_call(functools.partial(output_kernel, float(length)), out_shape...  1.19 us
  transfers between devices with their start and end apart: 1, of which 1 were waited for; matrix products, arithmetic and copies ran while one was open for 0% of the time, Pallas kernels for 2%

profile of v2, /device:TPU:24, one launch (start us, length us, event | category | flops | bytes accessed | tf_op | source)
XLA Modules:
  0.0 55.0 jit_solution(15567545336171772621)
XLA Ops:
  0.6 0.0 copy-start
  0.6 0.8 %copy-done = bf16[256,128]{1,0:T(8,128)(2,1)S(1)} copy-done((bf16[256,128]{1,0:T(8,128)(2,1)S(1)}, bf16[256,128]{1,0:T(8,128)(2,1)}, u32[]{:S(2)}) %copy-start) | copy-done | bytes 65560
  1.5 0.0 copy-start.2
  1.5 0.8 %copy-done.2 = bf16[256,128]{1,0:T(8,128)(2,1)S(1)} copy-done((bf16[256,128]{1,0:T(8,128)(2,1)S(1)}, bf16[256,128]{1,0:T(8,128)(2,1)}, u32[]{:S(2)}) %copy-start.2) | copy-done | bytes 65560
  2.3 0.0 copy-start.4
  2.3 0.8 %copy-done.4 = bf16[256,128]{1,0:T(8,128)(2,1)S(1)} copy-done((bf16[256,128]{1,0:T(8,128)(2,1)S(1)}, bf16[256,128]{1,0:T(8,128)(2,1)}, u32[]{:S(2)}) %copy-start.4) | copy-done | bytes 65560
  3.2 0.0 copy-start.6
  3.2 0.8 %copy-done.6 = bf16[256,128]{1,0:T(8,128)(2,1)S(1)} copy-done((bf16[256,128]{1,0:T(8,128)(2,1)S(1)}, bf16[256,128]{1,0:T(8,128)(2,1)}, u32[]{:S(2)}) %copy-start.6) | copy-done | bytes 65560
  4.0 0.0 copy-start.8
  4.0 0.7 %copy-done.8 = f32[256,16]{0,1:T(8,128)S(1)} copy-done((f32[256,16]{0,1:T(8,128)S(1)}, f32[256,16]{0,1:T(8,128)}, u32[]{:S(2)}) %copy-start.8) | copy-done | bytes 16408
  4.7 0.0 copy-start.5
  4.7 0.0 copy-start.7
  4.7 0.0 copy-start.9
  4.7 0.0 copy-start.10
  4.7 1.8 %chunk_summary.1 = bf16[256,128]{1,0:T(8,128)(2,1)} custom-call(bf16[256,128]{1,0:T(8,128)(2,1)S(1)} %copy-done, bf16[256,128]{1,0:T(8,128)(2,1)S(1)} %copy-done.2, bf16[256,128]{1,0:T(8,128)(2,1)S(1)} %copy-done.6, bf16[256,128]{1,0:T(8,128)(2,1)S(1)} %copy-done.4, f32[16,256]{1,0:T(8,128)S(1)} %bitcast.12), custom_call_target="tpu_custom_call" | custom-call | tf_op jit(solution)/shard_map/chunk_summary/pallas_call | solution.py:216
  6.5 0.0 copy-start.1
  6.5 0.0 copy-start.3
  6.5 16.5 %all-to-all-start = ((bf16[32,8,128]{2,1,0:T(8,128)(2,1)}), bf16[32,8,128]{2,1,0:T(8,128)(2,1)S(1)}, u32[]{:S(2)}, u32[]{:S(2)}) async-start(bf16[32,8,128]{2,1,0:T(8,128)(2,1)} %bitcast.1), calls=%async_computation | async-start | bytes 131072 | tf_op jit(solution)/shard_map/all_to_all | solution.py:213
  23.1 0.0 copy-done.5
  23.1 0.0 copy-done.7
  23.1 0.0 copy-done.9
  23.1 0.0 copy-done.10
  23.1 0.0 copy-done.1
  23.1 0.0 copy-done.3
  23.1 1.2 %local_part.1 = (f32[128,256]{1,0:T(8,128)S(1)}, f32[128,256]{1,0:T(8,128)S(1)}, f32[16,8,256]{2,1,0:T(8,128)S(1)}, f32[16,8,256]{2,1,0:T(8,128)S(1)}, f32[16,256]{1,0:T(8,128)S(1)}, /*index=5*/f32[8,128]{1,0:T(8,128)S(1)}) custom-call(s32[1]{0:T(128)} %bitcast.3.place_ref, bf16[256,128]{1,0:T(8,128)(2,1)S(1)} %copy-done.1, bf16[256,128]{1,0:T(8,128)(2,1)S(1)} %copy-done.3, ...), custom_call_target="tpu_custom_call" | custom-call | flops 20000000 | bytes 1500000 | tf_op jit(solution)/shard_map/local_part/pallas_call | solution.py:227
  24.4 12.4 %all-to-all-done = bf16[32,8,128]{2,1,0:T(8,128)(2,1)S(1)} async-done(((bf16[32,8,128]{2,1,0:T(8,128)(2,1)}), bf16[32,8,128]{2,1,0:T(8,128)(2,1)S(1)}, u32[]{:S(2)}, u32[]{:S(2)}) %all-to-all-start) | async-done | bytes 65568 | tf_op jit(solution)/shard_map/all_to_all | solution.py:213
  36.8 0.4 chunk_prefix.1
  37.2 16.7 %all_to_all.10 = bf16[32,8,128]{2,1,0:T(8,128)(2,1)S(1)} all-to-all(bf16[32,8,128]{2,1,0:T(8,128)(2,1)S(1)} %bitcast.11), channel_id=1, replica_groups=mesh['ctx'=32,'ch'=16] {'ctx'}, dimensions={0} | all-to-all | bytes 131072 | tf_op jit(solution)/shard_map/all_to_all | solution.py:213
  53.8 1.2 %outputs.1 = (bf16[256,128]{1,0:T(8,128)(2,1)}, bf16[256,128]{1,0:T(8,128)(2,1)}, bf16[256,128]{1,0:T(8,128)(2,1)}, f32[16,256]{1,0:T(8,128)}, f32[16,256]{1,0:T(8,128)}) custom-call(bf16[256,128]{1,0:T(8,128)(2,1)S(1)} %bitcast.9, f32[128,256]{1,0:T(8,128)S(1)} %get-tuple-element.17.conv_ref, f32[128,256]{1,0:T(8,128)S(1)} %get-tuple-element.18.back_ref, ...), custom_call_target="tpu_custom_call" | custom-call | tf_op jit(solution)/shard_map/outputs/pallas_call | solution.py:255
Async XLA Ops:
  0.6 0.8 %copy-start = (bf16[256,128]{1,0:T(8,128)(2,1)S(1)}, bf16[256,128]{1,0:T(8,128)(2,1)}, u32[]{:S(2)}) copy-start(bf16[256,128]{1,0:T(8,128)(2,1)} %key_ref.5) | copy-start | bytes 196612
  1.5 0.8 %copy-start.2 = (bf16[256,128]{1,0:T(8,128)(2,1)S(1)}, bf16[256,128]{1,0:T(8,128)(2,1)}, u32[]{:S(2)}) copy-start(bf16[256,128]{1,0:T(8,128)(2,1)} %value_ref.5) | copy-start | bytes 196612
  2.3 0.8 %copy-start.4 = (bf16[256,128]{1,0:T(8,128)(2,1)S(1)}, bf16[256,128]{1,0:T(8,128)(2,1)}, u32[]{:S(2)}) copy-start(bf16[256,128]{1,0:T(8,128)(2,1)} %out_grad_ref.5) | copy-start | bytes 196612
  3.2 0.8 %copy-start.6 = (bf16[256,128]{1,0:T(8,128)(2,1)S(1)}, bf16[256,128]{1,0:T(8,128)(2,1)}, u32[]{:S(2)}) copy-start(bf16[256,128]{1,0:T(8,128)(2,1)} %query_ref.3) | copy-start | bytes 196612
  4.0 0.7 %copy-start.8 = (f32[256,16]{0,1:T(8,128)S(1)}, f32[256,16]{0,1:T(8,128)}, u32[]{:S(2)}) copy-start(f32[256,16]{0,1:T(8,128)} %param.11) | copy-start | bytes 49156
  4.7 18.3 %copy-start.5 = (bf16[256,128]{1,0:T(8,128)(2,1)S(1)}, bf16[256,128]{1,0:T(8,128)(2,1)}, u32[]{:S(2)}) copy-start(bf16[256,128]{1,0:T(8,128)(2,1)} %out_grad_ref.5) | copy-start | bytes 196612
  4.7 18.4 %copy-start.7 = (bf16[256,128]{1,0:T(8,128)(2,1)S(1)}, bf16[256,128]{1,0:T(8,128)(2,1)}, u32[]{:S(2)}) copy-start(bf16[256,128]{1,0:T(8,128)(2,1)} %query_ref.3) | copy-start | bytes 196612
  4.7 18.4 %copy-start.9 = (f32[256,16]{0,1:T(8,128)S(1)}, f32[256,16]{0,1:T(8,128)}, u32[]{:S(2)}) copy-start(f32[256,16]{0,1:T(8,128)} %param.11) | copy-start | bytes 49156
  4.7 18.4 %copy-start.10 = (f32[256,16]{0,1:T(8,128)S(1)}, f32[256,16]{0,1:T(8,128)}, u32[]{:S(2)}) copy-start(f32[256,16]{0,1:T(8,128)} %param.10) | copy-start | bytes 49156
  6.5 16.6 %copy-start.1 = (bf16[256,128]{1,0:T(8,128)(2,1)S(1)}, bf16[256,128]{1,0:T(8,128)(2,1)}, u32[]{:S(2)}) copy-start(bf16[256,128]{1,0:T(8,128)(2,1)} %key_ref.5) | copy-start | bytes 196612
  6.5 16.6 %copy-start.3 = (bf16[256,128]{1,0:T(8,128)(2,1)S(1)}, bf16[256,128]{1,0:T(8,128)(2,1)}, u32[]{:S(2)}) copy-start(bf16[256,128]{1,0:T(8,128)(2,1)} %value_ref.5) | copy-start | bytes 196612
  6.5 30.3 %all-to-all-start = ((bf16[32,8,128]{2,1,0:T(8,128)(2,1)}), bf16[32,8,128]{2,1,0:T(8,128)(2,1)S(1)}, u32[]{:S(2)}, u32[]{:S(2)}) async-start(bf16[32,8,128]{2,1,0:T(8,128)(2,1)} %bitcast.1), calls=%async_computation | async-start | bytes 131072 | tf_op jit(solution)/shard_map/all_to_all | solution.py:213

commit v3 on v2

--- a/solution.py
+++ b/solution.py
@@ -12,6 +12,7 @@
 POLES = 16
 BLOCK = 8
 LANES = 128
+MIB = 1024 * 1024
 
 
 def gated(left_ref, right_ref):
@@ -23,10 +24,25 @@
     return value.astype(BF16).astype(F32)
 
 
-def summary_kernel(length, key_ref, value_ref, query_ref, out_grad_ref, log_ref, out_ref, mixed, grad):
+def load_gates(sources, held, sems, mixed, grad):
+    copies = [pltpu.make_async_copy(src, dst, sems.at[n]) for n, (src, dst) in enumerate(zip(sources, held))]
+    for copy in copies:
+        copy.start()
+    copies[0].wait()
+    copies[1].wait()
+    mixed[...] = gated(held[0], held[1])
+    copies[2].wait()
+    copies[3].wait()
+    grad[...] = gated(held[2], held[3])
+    for copy in copies[4:]:
+        copy.wait()
+
+
+def summary_kernel(length, *refs):
+    sources, (out_ref, mixed, grad, sems), held = refs[:5], refs[5:9], refs[9:]
+    load_gates(sources, held, sems, mixed, grad)
+    log_ref = held[4]
     width, channels = mixed.shape
-    mixed[...] = gated(key_ref, value_ref)
-    grad[...] = gated(query_ref, out_grad_ref)
     decay = jnp.exp(-(jnp.exp(log_ref[...]) / length))
     zero = jnp.zeros((POLES, channels), F32)
 
@@ -55,28 +71,12 @@
     out_ref[...] = jnp.concatenate(rows, axis=0).T.astype(BF16)
 
 
-def local_kernel(
-    length,
-    place_ref,
-    key_ref,
-    value_ref,
-    query_ref,
-    out_grad_ref,
-    residue_ref,
-    log_ref,
-    conv_ref,
-    back_ref,
-    ahead_ref,
-    behind_ref,
-    fade_ref,
-    chunk_ref,
-    mixed,
-    grad,
-    logs,
-):
+def local_kernel(length, places, index_ref, *refs):
+    sources, outs, (mixed, grad, logs, sems), held = refs[:6], refs[6:12], refs[12:16], refs[16:]
+    load_gates(sources, held, sems, mixed, grad)
+    log_ref, residue_ref = held[4:]
+    conv_ref, back_ref, ahead_ref, behind_ref, fade_ref, chunk_ref = outs
     width, channels = mixed.shape
-    mixed[...] = gated(key_ref, value_ref)
-    grad[...] = gated(query_ref, out_grad_ref)
     rates = jnp.exp(log_ref[...]) / length
     decay = jnp.exp(-rates)
     weight = residue_ref[...] * (length**-0.5)
@@ -105,11 +105,14 @@
         behind_ref[pole] = scale * jnp.exp(-(rate * (BLOCK - steps)))
     fade_ref[...] = jnp.exp(-(rates * BLOCK))
     logs[...] = jnp.concatenate([log_ref[...]] * (LANES // POLES), axis=0).T
-    own = logs[pl.ds(pl.multiple_of(place_ref[0] * BLOCK, BLOCK), BLOCK), :]
+    place = 0
+    for member, at in enumerate(places):
+        place = jnp.where(index_ref[0] == member, at, place)
+    own = logs[pl.ds(pl.multiple_of(place * BLOCK, BLOCK), BLOCK), :]
     chunk_ref[...] = jnp.exp(-(jnp.exp(own) / length * width))
 
 
-def prefix_kernel(width, parts_ref, chunk_ref, out_ref):
+def prefix_kernel(width, places, parts_ref, chunk_ref, out_ref):
     chunks = parts_ref.shape[0] // BLOCK
     fade = chunk_ref[...]
     lane = lax.broadcasted_iota(jnp.int32, fade.shape, 1)
@@ -122,6 +125,7 @@
     for pair in range(chunks // 2):
         both = parts_ref[pair * 2 * BLOCK : (pair + 1) * 2 * BLOCK, :].astype(F32)
         parts += [both[:BLOCK], both[BLOCK:]]
+    parts = [parts[at] for at in places]
     ends = [part + shifted(part, 6) for part in parts]
     state, moment, res, rate = zero, zero, zero, zero
     states = []
@@ -142,8 +146,11 @@
         rest = pltpu.roll(whole - rounded(whole), LANES // 2, 1)
         sent[chunk] = jnp.where(lane < LANES // 2, whole, rest)
         back = fade * back + ends[chunk]
+    placed = [None] * chunks
+    for chunk, at in enumerate(places):
+        placed[at] = sent[chunk]
     for pair in range(chunks // 2):
-        both = jnp.concatenate(sent[2 * pair : 2 * pair + 2], axis=0)
+        both = jnp.concatenate(placed[2 * pair : 2 * pair + 2], axis=0)
         out_ref[pair * 2 * BLOCK : (pair + 1) * 2 * BLOCK, :] = both.astype(BF16)
 
 
@@ -158,8 +165,8 @@
     key_ref,
     value_ref,
     out_grad_ref,
+    log_ref,
     residue_ref,
-    log_ref,
     query_out,
     key_out,
     value_out,
@@ -196,6 +203,10 @@
         value_out[here, :] = (back * key_ref[here, :].astype(F32)).astype(BF16)
 
 
+def member_order(chunks):
+    return [(place + chunks // 2) % chunks for place in range(chunks)]
+
+
 def on_device(query, key_gate, value_in, grad_output, residue, log_rate):
     chunks = lax.axis_size("ctx")
     channels, width = query.shape
@@ -203,29 +214,35 @@
     struct = jax.ShapeDtypeStruct
     in_vmem = pl.BlockSpec(memory_space=pltpu.VMEM)
     turned = [pltpu.VMEM((width, channels), F32)] * 2
-    params = pltpu.CompilerParams(vmem_limit_bytes=32 * 1024 * 1024)
-    gates = (key_gate, value_in, query, grad_output)
-    poles = (residue.T, log_rate.T)
+    held = [pltpu.VMEM((channels, width), BF16)] * 4 + [pltpu.VMEM((POLES, channels), F32)] * 2
+    params = pltpu.CompilerParams(vmem_limit_bytes=32 * MIB)
+    poles = (log_rate.T, residue.T)
+    sources = [pltpu.with_memory_space_constraint(x, pltpu.HBM) for x in (key_gate, value_in, query, grad_output, *poles)]
+    in_hbm = pl.BlockSpec(memory_space=pltpu.HBM)
     sent = struct((channels, LANES), BF16)
     per_chunk = (chunks, channels // chunks, LANES)
+    order = member_order(chunks)
+    places = [order.index(member) for member in range(chunks)]
 
     def exchange(table):
-        table = lax.all_to_all(table.reshape(per_chunk), "ctx", split_axis=0, concat_axis=0, tiled=True)
+        table = lax.all_to_all(
+            table.reshape(per_chunk), "ctx", split_axis=0, concat_axis=0, axis_index_groups=[order], tiled=True
+        )
         return table.reshape(channels, LANES)
 
     summary = pl.pallas_call(
         functools.partial(summary_kernel, float(length)),
         out_shape=sent,
-        in_specs=[in_vmem] * 5,
+        in_specs=[in_hbm] * 5,
         out_specs=in_vmem,
-        scratch_shapes=turned,
+        scratch_shapes=[*turned, pltpu.SemaphoreType.DMA((5,)), *held[:5]],
         compiler_params=params,
         name="chunk_summary",
-    )(*gates, poles[1])
+    )(*sources[:5])
     parts = exchange(summary)
-    place = lax.axis_index("ctx").astype(jnp.int32).reshape(1)
+    index = lax.axis_index("ctx").astype(jnp.int32).reshape(1)
     conv, back, ahead, behind, fade, chunk_fade = pl.pallas_call(
-        functools.partial(local_kernel, float(length)),
+        functools.partial(local_kernel, float(length), places),
         out_shape=(
             struct((width, channels), F32),
             struct((width, channels), F32),
@@ -234,15 +251,15 @@
             struct((POLES, channels), F32),
             struct((BLOCK, LANES), F32),
         ),
-        in_specs=[pl.BlockSpec(memory_space=pltpu.SMEM)] + [in_vmem] * 6,
+        in_specs=[pl.BlockSpec(memory_space=pltpu.SMEM)] + [in_hbm] * 6,
         out_specs=[in_vmem] * 6,
-        scratch_shapes=turned + [pltpu.VMEM((channels, LANES), F32)],
+        scratch_shapes=[*turned, pltpu.VMEM((channels, LANES), F32), pltpu.SemaphoreType.DMA((6,)), *held],
         compiler_params=params,
         name="local_part",
         cost_estimate=pl.CostEstimate(flops=20_000_000, bytes_accessed=1_500_000, transcendentals=0),
-    )(place, *gates, *poles)
+    )(index, *sources)
     carried = pl.pallas_call(
-        functools.partial(prefix_kernel, float(width)),
+        functools.partial(prefix_kernel, float(width), places),
         out_shape=sent,
         in_specs=[in_vmem] * 2,
         out_specs=in_vmem,

time: 55.5 us -> 46.6 us (0.84)
  waiting for transfers between devices: 12.4 us -> 2.16 us
  local copies, waits for them, and re-layouts: 4.09 us -> 0.02 us
  starting transfers between devices: 16.5 us -> 19.9 us
  Pallas kernels: 4.61 us -> 6.71 us
    all_to_all x1, waiting for transfers between devices: 12.4 us -> 2.16 us  [exchange(): lax.all_to_all(table.reshape(per_chunk), 'ctx', split_axis=0, concat_axis...]
    unnamed x22 -> x10, local copies, waits for them, and re-layouts: 4.09 us -> 0.02 us
    all_to_all x1, starting transfers between devices: 16.5 us -> 19.9 us  [exchange(): lax.all_to_all(table.reshape(per_chunk), 'ctx', split_axis=0, concat_axis...]
    pallas_call x2, Pallas kernels: 1.65 us -> 2.7 us  [the longest x1 2.3 us: on_device(): pl.pallas_call(functools.partial(local_kernel, float(length), places), ou...]
    pallas_call x1, Pallas kernels: 1.77 us -> 2.81 us  [on_device(): pl.pallas_call(functools.partial(summary_kernel, float(length)), out_shap...]
  transfers between devices with their start and end apart: 1 -> 1, of which waited for: 1 -> 1; matrix products, arithmetic and copies ran while one was open for 0% -> 0% of each run, Pallas kernels for 2% -> 5%
where the time goes in v3:
time: 46.6 us; the launch traced here: 46.3 us
  starting transfers between devices  19.9 us (43%)
  blocking collectives  16.7 us (36%)
  Pallas kernels  6.71 us (14%)
  waiting for transfers between devices  2.16 us (5%)
  between operations  0.7 us (2%)
    all_to_all x1, starting transfers between devices, exchange(): lax.all_to_all(table.reshape(per_chunk), 'ctx', split_axis=0, concat_axis...  19.9 us
    all_to_all x1, blocking collectives, exchange(): lax.all_to_all(table.reshape(per_chunk), 'ctx', split_axis=0, concat_axis...  16.7 us
    pallas_call x1, Pallas kernels, on_device(): pl.pallas_call(functools.partial(summary_kernel, float(length)), out_shap...  2.81 us
    pallas_call x1, Pallas kernels, on_device(): pl.pallas_call(functools.partial(local_kernel, float(length), places), ou...  2.3 us
    all_to_all x1, waiting for transfers between devices, exchange(): lax.all_to_all(table.reshape(per_chunk), 'ctx', split_axis=0, concat_axis...  2.16 us
    pallas_call x1, Pallas kernels, on_device(): pl.pallas_call(functools.partial(output_kernel, float(length)), out_shape...  1.2 us
  transfers between devices with their start and end apart: 1, of which 1 were waited for; matrix products, arithmetic and copies ran while one was open for 0% of the time, Pallas kernels for 5%

profile of v3, /device:TPU:24, one launch (start us, length us, event | category | flops | bytes accessed | tf_op | source)
XLA Modules:
  0.0 46.3 jit_solution(10217434454160233035)
XLA Ops:
  0.6 2.8 %chunk_summary.1 = bf16[256,128]{1,0:T(8,128)(2,1)} custom-call(bf16[256,128]{1,0:T(8,128)(2,1)} %key_ref.1, bf16[256,128]{1,0:T(8,128)(2,1)} %value_ref.1, bf16[256,128]{1,0:T(8,128)(2,1)} %refs_2_.3, bf16[256,128]{1,0:T(8,128)(2,1)} %out_grad_ref.1, f32[16,256]{1,0:T(8,128)} %bitcast.12), custom_call_target="tpu_custom_call" | custom-call | tf_op jit(solution)/shard_map/chunk_summary/pallas_call | solution.py:233
  3.4 19.9 %all-to-all-start = ((bf16[32,8,128]{2,1,0:T(8,128)(2,1)}), bf16[32,8,128]{2,1,0:T(8,128)(2,1)S(1)}, u32[]{:S(2)}, u32[]{:S(2)}) async-start(bf16[32,8,128]{2,1,0:T(8,128)(2,1)} %bitcast.1), calls=%async_computation | async-start | bytes 131072 | tf_op jit(solution)/shard_map/all_to_all | solution.py:228
  23.4 2.3 %local_part.1 = (f32[128,256]{1,0:T(8,128)S(1)}, f32[128,256]{1,0:T(8,128)S(1)}, f32[16,8,256]{2,1,0:T(8,128)S(1)}, f32[16,8,256]{2,1,0:T(8,128)S(1)}, f32[16,256]{1,0:T(8,128)S(1)}, /*index=5*/f32[8,128]{1,0:T(8,128)S(1)}) custom-call(s32[1]{0:T(128)} %bitcast.3.index_ref, bf16[256,128]{1,0:T(8,128)(2,1)} %key_ref.1, bf16[256,128]{1,0:T(8,128)(2,1)} %value_ref.1, ...), custom_call_target="tpu_custom_call" | custom-call | flops 20000000 | bytes 1500000 | tf_op jit(solution)/shard_map/local_part/pallas_call | solution.py:244
  25.7 2.2 %all-to-all-done = bf16[32,8,128]{2,1,0:T(8,128)(2,1)S(1)} async-done(((bf16[32,8,128]{2,1,0:T(8,128)(2,1)}), bf16[32,8,128]{2,1,0:T(8,128)(2,1)S(1)}, u32[]{:S(2)}, u32[]{:S(2)}) %all-to-all-start) | async-done | bytes 65568 | tf_op jit(solution)/shard_map/all_to_all | solution.py:228
  27.9 0.0 copy-start.2
  27.9 0.0 copy-start.3
  27.9 0.0 copy-start.4
  27.9 0.4 chunk_prefix.1
  28.3 0.0 copy-start
  28.3 0.0 copy-start.1
  28.3 16.7 %all_to_all.10 = bf16[32,8,128]{2,1,0:T(8,128)(2,1)S(1)} all-to-all(bf16[32,8,128]{2,1,0:T(8,128)(2,1)S(1)} %bitcast.11), channel_id=1, replica_groups={{256,272,288,304,320,336,352,368,384,400,416,432,448,464,480,496,0,16,3..., dimensions={0} | all-to-all | bytes 131072 | tf_op jit(solution)/shard_map/all_to_all | solution.py:228
  45.0 0.0 copy-done.2
  45.1 0.0 copy-done.3
  45.1 0.0 copy-done.4
  45.1 0.0 copy-done
  45.1 0.0 copy-done.1
  45.1 1.2 %outputs.1 = (bf16[256,128]{1,0:T(8,128)(2,1)}, bf16[256,128]{1,0:T(8,128)(2,1)}, bf16[256,128]{1,0:T(8,128)(2,1)}, f32[16,256]{1,0:T(8,128)}, f32[16,256]{1,0:T(8,128)}) custom-call(bf16[256,128]{1,0:T(8,128)(2,1)S(1)} %bitcast.9, f32[128,256]{1,0:T(8,128)S(1)} %get-tuple-element.17.conv_ref, f32[128,256]{1,0:T(8,128)S(1)} %get-tuple-element.18.back_ref, ...), custom_call_target="tpu_custom_call" | custom-call | tf_op jit(solution)/shard_map/outputs/pallas_call | solution.py:272
Async XLA Ops:
  3.4 24.4 %all-to-all-start = ((bf16[32,8,128]{2,1,0:T(8,128)(2,1)}), bf16[32,8,128]{2,1,0:T(8,128)(2,1)S(1)}, u32[]{:S(2)}, u32[]{:S(2)}) async-start(bf16[32,8,128]{2,1,0:T(8,128)(2,1)} %bitcast.1), calls=%async_computation | async-start | bytes 131072 | tf_op jit(solution)/shard_map/all_to_all | solution.py:228
  27.9 17.2 %copy-start.2 = (bf16[256,128]{1,0:T(8,128)(2,1)S(1)}, bf16[256,128]{1,0:T(8,128)(2,1)}, u32[]{:S(2)}) copy-start(bf16[256,128]{1,0:T(8,128)(2,1)} %out_grad_ref.1) | copy-start | bytes 196612
  27.9 17.2 %copy-start.3 = (f32[256,16]{0,1:T(8,128)S(1)}, f32[256,16]{0,1:T(8,128)}, u32[]{:S(2)}) copy-start(f32[256,16]{0,1:T(8,128)} %param.11) | copy-start | bytes 49156
  27.9 17.2 %copy-start.4 = (f32[256,16]{0,1:T(8,128)S(1)}, f32[256,16]{0,1:T(8,128)}, u32[]{:S(2)}) copy-start(f32[256,16]{0,1:T(8,128)} %param.10) | copy-start | bytes 49156
  28.3 16.8 %copy-start = (bf16[256,128]{1,0:T(8,128)(2,1)S(1)}, bf16[256,128]{1,0:T(8,128)(2,1)}, u32[]{:S(2)}) copy-start(bf16[256,128]{1,0:T(8,128)(2,1)} %key_ref.1) | copy-start | bytes 196612
  28.3 16.8 %copy-start.1 = (bf16[256,128]{1,0:T(8,128)(2,1)S(1)}, bf16[256,128]{1,0:T(8,128)(2,1)}, u32[]{:S(2)}) copy-start(bf16[256,128]{1,0:T(8,128)(2,1)} %value_ref.1) | copy-start | bytes 196612

commit v4 on v3

v4 whole, which is shorter than its diff:
```python
import functools

import jax
import jax.numpy as jnp
from jax import lax
from jax.experimental import pallas as pl
from jax.experimental.pallas import tpu as pltpu
from jax.sharding import PartitionSpec as P

F32 = jnp.float32
BF16 = jnp.bfloat16
POLES = 16
BLOCK = 8
LANES = 128
NEAR = 4
EARLY = 8
MIB = 1024 * 1024


def gated(left_ref, right_ref):
    product = (left_ref[...].astype(F32) * right_ref[...].astype(F32)).astype(BF16)
    return product.astype(F32).T


def crossed(first, second):
    left = lax.broadcasted_iota(jnp.int32, first.shape, 1) < LANES // 2
    return (
        jnp.where(left, first, pltpu.roll(second, LANES // 2, 1)),
        jnp.where(left, pltpu.roll(first, LANES // 2, 1), second),
    )


def unpacked(block):
    low = pltpu.roll(block, LANES // 2, 1)
    return [half[at * POLES : (at + 1) * POLES] for half in (block, low) for at in range(3)]


def joined(parts, fade, width):
    zero = jnp.zeros(fade.shape, F32)
    state, moment, res, rate = zero, zero, zero, zero
    ahead, behind = [], []
    for end, start, end_moment, start_moment, part_res, part_rate in parts:
        ahead.append(state)
        res = res + part_res + start * state
        rate = rate + part_rate + start_moment * state + start * moment
        moment = fade * (moment + width * state) + end_moment
        state = fade * state + end
    back, back_moment = zero, zero
    for _, start, _, start_moment, _, _ in parts[::-1]:
        behind.append(back)
        back_moment = fade * (back_moment + width * back) + start_moment
        back = fade * back + start
    return (state, back, moment, back_moment, res, rate), ahead, behind[::-1]


def own_rates(length, near, index, log_ref):
    block = near - 1 - lax.rem(index, near)
    logs = jnp.where(block >= 2, log_ref[:, LANES:], log_ref[:, :LANES])
    logs = jnp.where(lax.rem(block, 2) == 1, pltpu.roll(logs, LANES // 2, 1), logs)
    return jnp.exp(logs) / length


def load_gates(sources, held, sems, mixed, grad):
    copies = [pltpu.make_async_copy(src, dst, sems.at[n]) for n, (src, dst) in enumerate(zip(sources, held))]
    for copy in copies:
        copy.start()
    copies[0].wait()
    copies[1].wait()
    mixed[...] = gated(held[0], held[1])
    copies[2].wait()
    copies[3].wait()
    grad[...] = gated(held[2], held[3])
    for copy in copies[4:]:
        copy.wait()


def summary_kernel(length, index_ref, *refs):
    sources, out_ref, held, (mixed, grad, sems) = refs[:6], refs[6], refs[7:13], refs[13:]
    load_gates(sources, held, sems, mixed, grad)
    log_ref = held[4]
    width, channels = mixed.shape
    decay = jnp.exp(-(jnp.exp(log_ref[...]) / length))
    zero = jnp.zeros((POLES, channels), F32)

    def step(block, carry):
        state, moment, res, rate, back, back_moment = carry
        first = block * BLOCK
        for row in range(BLOCK):
            mixed_row = mixed[pl.ds(first + row, 1), :]
            grad_row = grad[pl.ds(first + row, 1), :]
            late_row = grad[pl.ds(width - 1 - first - row, 1), :]
            faded = decay * state
            state = faded + mixed_row
            moment = decay * moment + faded
            res = res + grad_row * state
            rate = rate + grad_row * moment
            faded = decay * back
            back = faded + late_row
            back_moment = decay * back_moment + faded
        return state, moment, res, rate, back, back_moment

    state, moment, res, rate, back, back_moment = lax.fori_loop(0, width // BLOCK, step, (zero,) * 6)
    last = decay * state
    last_moment = decay * moment + last
    top = jnp.concatenate([last, back, last_moment], axis=0)
    low = jnp.concatenate([back_moment, res, rate], axis=0)
    rows = top.shape[0]
    for half in range(channels // LANES):
        here = slice(half * LANES, (half + 1) * LANES)
        pair = crossed(top[:, here], low[:, here])
        for side in range(2):
            block = 2 * half + side
            out_ref[block * rows : (block + 1) * rows, :] = pair[side]


def local_part(length, mixed, grad, log_ref, residue_ref, conv_ref, back_ref, ahead_ref, behind_ref, fade_ref):
    width, channels = mixed.shape
    rates = jnp.exp(log_ref[...]) / length
    decay = jnp.exp(-rates)
    weight = residue_ref[...] * (length**-0.5)
    zero = jnp.zeros((POLES, channels), F32)

    def step(block, carry):
        state, back = carry
        first = pl.multiple_of(block * BLOCK, BLOCK)
        last = pl.multiple_of(width - BLOCK - block * BLOCK, BLOCK)
        ahead, behind = [], []
        for row in range(BLOCK):
            state = decay * state + mixed[pl.ds(first + row, 1), :]
            ahead.append(jnp.sum(weight * state, axis=0, keepdims=True))
            back = decay * back + grad[pl.ds(last + BLOCK - 1 - row, 1), :]
            behind.append(jnp.sum(weight * back, axis=0, keepdims=True))
        conv_ref[pl.ds(first, BLOCK), :] = jnp.concatenate(ahead, axis=0)
        back_ref[pl.ds(last, BLOCK), :] = jnp.concatenate(behind[::-1], axis=0)
        return state, back

    lax.fori_loop(0, width // BLOCK, step, (zero, zero))
    steps = lax.broadcasted_iota(jnp.int32, (BLOCK, channels), 0).astype(F32)
    for pole in range(POLES):
        rate = rates[pole : pole + 1]
        scale = weight[pole : pole + 1]
        ahead_ref[pole] = scale * jnp.exp(-(rate * steps))
        behind_ref[pole] = scale * jnp.exp(-(rate * (BLOCK - steps)))
    fade_ref[...] = jnp.exp(-(rates * BLOCK))


def group_kernel(length, width, near, index_ref, parts_ref, mixed, grad, log_ref, residue_ref, out_ref, *tables):
    rows = 3 * POLES

    @pl.when(index_ref[0] < EARLY)
    def _():
        local_part(length, mixed, grad, log_ref, residue_ref, *tables)

    fade = jnp.exp(-(own_rates(length, near, index_ref[0], log_ref) * width))
    parts = [unpacked(parts_ref[at * rows : (at + 1) * rows, :]) for at in range(near - 1, -1, -1)]
    whole, _, _ = joined(parts, fade, width)
    end, start, end_moment, start_moment, res, rate = whole
    top = jnp.concatenate([end, start, end_moment], axis=0)
    low = jnp.concatenate([start_moment, res, rate], axis=0)
    sent = crossed(top, low)[0].astype(BF16)
    for at in range(out_ref.shape[0] // rows):
        out_ref[at * rows : (at + 1) * rows, :] = sent


def total_kernel(length, width, near, far_order, index_ref, parts_ref, groups_ref, log_ref, out_ref):
    rows = 3 * POLES
    index = index_ref[0]
    group = lax.div(index, near)
    rates = own_rates(length, near, index, log_ref)
    fade = jnp.exp(-(rates * width))
    groups = [None] * len(far_order)
    for at, member in enumerate(far_order):
        groups[member] = unpacked(groups_ref[at * rows : (at + 1) * rows, :].astype(F32))
    whole, ahead, behind = joined(groups, jnp.exp(-(rates * (width * near))), width * near)
    state, back = ahead[0], behind[0]
    for member in range(1, len(groups)):
        state = jnp.where(group == member, ahead[member], state)
        back = jnp.where(group == member, behind[member], back)
    states, backs = [], []
    for chunk in range(near):
        block = parts_ref[(near - 1 - chunk) * rows : (near - chunk) * rows, :]
        states.append(state)
        state = fade * state + block[:POLES]
    for chunk in range(near - 1, -1, -1):
        block = parts_ref[(near - 1 - chunk) * rows : (near - chunk) * rows, :]
        backs.append(back)
        back = fade * back + block[POLES : 2 * POLES]
    totals = jnp.concatenate(whole[4:], axis=0)
    rows = 2 * POLES
    for at in range(near):
        entering = jnp.concatenate([states[near - 1 - at], backs[at]], axis=0)
        out_ref[at * rows : (at + 1) * rows, :] = crossed(entering, totals)[0]


def output_kernel(length, index_ref, carried_ref, *refs):
    early, (key_ref, value_ref, out_grad_ref, log_ref, residue_ref, mixed, grad), outs, late = (
        refs[:5],
        refs[5:12],
        refs[12:17],
        refs[17:],
    )
    residue_out, log_out = outs[3:]
    channels = residue_ref.shape[1]
    rates = jnp.exp(log_ref[...]) / length
    rate_scale = -(residue_ref[...] / length) * rates
    size = 2 * POLES
    states = []
    for half in range(channels // LANES):
        here = slice(half * LANES, (half + 1) * LANES)
        first, second = (carried_ref[at * size : (at + 1) * size, :] for at in (2 * half, 2 * half + 1))
        entering, totals = crossed(first, second)
        states.append(entering)
        residue_out[:, here] = totals[:POLES] * (1.0 / length)
        log_out[:, here] = rate_scale[:, here] * totals[POLES:]

    @pl.when(index_ref[0] < EARLY)
    def _():
        gate_gradients(states, early, key_ref, value_ref, out_grad_ref, *outs[:3])

    @pl.when(index_ref[0] >= EARLY)
    def _():
        local_part(length, mixed, grad, log_ref, residue_ref, *late)
        gate_gradients(states, late, key_ref, value_ref, out_grad_ref, *outs[:3])


def gate_gradients(states, tables, key_ref, value_ref, out_grad_ref, query_out, key_out, value_out):
    conv_ref, back_ref, ahead_ref, behind_ref, fade_ref = tables
    blocks = conv_ref.shape[0] // BLOCK
    for half, entering in enumerate(states):
        here = slice(half * LANES, (half + 1) * LANES)
        total = [conv_ref[block * BLOCK : (block + 1) * BLOCK, here] for block in range(blocks)]
        for pole in range(POLES):
            term = ahead_ref[pole, :, here] * entering[pole : pole + 1]
            fade = fade_ref[pole : pole + 1, here]
            for block in range(blocks):
                total[block] = total[block] + term
                term = term * fade
        conv = jnp.concatenate(total, axis=0).T.astype(BF16).astype(F32)
        query_out[here, :] = (out_grad_ref[here, :].astype(F32) * conv).astype(BF16)
        total = [back_ref[block * BLOCK : (block + 1) * BLOCK, here] for block in range(blocks)]
        for pole in range(POLES):
            term = behind_ref[pole, :, here] * entering[POLES + pole : POLES + pole + 1]
            fade = fade_ref[pole : pole + 1, here]
            for block in range(blocks - 1, -1, -1):
                total[block] = total[block] + term
                term = term * fade
        back = jnp.concatenate(total, axis=0).T.astype(BF16).astype(F32)
        key_out[here, :] = (back * value_ref[here, :].astype(F32)).astype(BF16)
        value_out[here, :] = (back * key_ref[here, :].astype(F32)).astype(BF16)


def on_device(query, key_gate, value_in, grad_output, residue, log_rate):
    chunks = lax.axis_size("ctx")
    channels, width = query.shape
    length = width * chunks
    struct = jax.ShapeDtypeStruct
    in_vmem = pl.BlockSpec(memory_space=pltpu.VMEM)
    in_smem = pl.BlockSpec(memory_space=pltpu.SMEM)
    in_hbm = pl.BlockSpec(memory_space=pltpu.HBM)
    params = pltpu.CompilerParams(vmem_limit_bytes=32 * MIB)
    gate, pole = struct((channels, width), BF16), struct((POLES, channels), F32)
    turned = struct((width, channels), F32)
    spread = struct((POLES, BLOCK, channels), F32)
    sources = [key_gate, value_in, query, grad_output, log_rate.T, residue.T]
    sources = [pltpu.with_memory_space_constraint(source, pltpu.HBM) for source in sources]
    tables = (turned, turned, spread, spread, pole)
    index = lax.axis_index("ctx").astype(jnp.int32).reshape(1)
    near, far = NEAR, chunks // NEAR
    rows = 3 * POLES
    far_order = [(5 * far // 8 - place) % far for place in range(far)]
    near_groups = [[group * near + near - 1 - place for place in range(near)] for group in range(far)]
    far_groups = [[group * near + member for group in far_order] for member in range(near)]

    def exchange(table, groups):
        members = len(groups[0])
        shape = table.shape
        table = table.reshape(members, shape[0] // members, LANES)
        table = lax.all_to_all(table, "ctx", split_axis=0, concat_axis=0, axis_index_groups=groups, tiled=True)
        return table.reshape(shape)

    summary, key_gate, value_in, _, grad_output, logs, residues, mixed, grad = pl.pallas_call(
        functools.partial(summary_kernel, float(length)),
        out_shape=(struct((near * rows, LANES), F32), gate, gate, gate, gate, pole, pole, turned, turned),
        in_specs=[in_smem] + [in_hbm] * 6,
        out_specs=[in_vmem] * 9,
        scratch_shapes=[pltpu.SemaphoreType.DMA((6,))],
        compiler_params=params,
        name="chunk_summary",
    )(index, *sources)
    parts = exchange(summary, near_groups)
    group, *early = pl.pallas_call(
        functools.partial(group_kernel, float(length), float(width), near),
        out_shape=(struct((far * rows, LANES), BF16), *tables),
        in_specs=[in_smem] + [in_vmem] * 5,
        out_specs=[in_vmem] * 6,
        compiler_params=params,
        name="group_summary",
    )(index, parts, mixed, grad, logs, residues)
    groups = exchange(group, far_groups)
    carried = pl.pallas_call(
        functools.partial(total_kernel, float(length), float(width), near, far_order),
        out_shape=struct((near * 2 * POLES, LANES), F32),
        in_specs=[in_smem, in_vmem, in_vmem, in_vmem],
        out_specs=in_vmem,
        compiler_params=params,
        name="totals",
    )(index, parts, groups, logs)
    carried = exchange(carried, near_groups)
    outs = pl.pallas_call(
        functools.partial(output_kernel, float(length)),
        out_shape=(gate, gate, gate, pole, pole),
        in_specs=[in_smem] + [in_vmem] * 13,
        out_specs=[in_vmem] * 5,
        scratch_shapes=[pltpu.VMEM(table.shape, table.dtype) for table in tables],
        compiler_params=params,
        name="outputs",
    )(index, carried, *early, key_gate, value_in, grad_output, logs, residues, mixed, grad)
    return (*outs[:3], outs[3].T, outs[4].T)


def solution(mesh):
    both = P("ch", "ctx")
    rows = P("ch", None)
    return jax.shard_map(
        on_device,
        mesh=mesh,
        in_specs=(both, both, both, both, rows, rows),
        out_specs=(both, both, both, rows, rows),
        check_vma=False,
    )
```

time: 46.6 us -> 41.1 us (0.88)
  starting transfers between devices: 19.9 us -> 0 us
  blocking collectives: 16.7 us -> 34.8 us
  waiting for transfers between devices: 2.16 us -> 0 us
  Pallas kernels: 6.71 us -> 5.41 us
    all_to_all x1 -> x0, starting transfers between devices: 19.9 us -> none  [exchange(): lax.all_to_all(table.reshape(per_chunk), 'ctx', split_axis=0, concat_axis...]
    all_to_all x1 -> x3, blocking collectives: 16.7 us -> 34.8 us  [exchange(): lax.all_to_all(table, 'ctx', split_axis=0, concat_axis=0, axis_index_grou...]
    all_to_all x1 -> x0, waiting for transfers between devices: 2.16 us -> none  [exchange(): lax.all_to_all(table.reshape(per_chunk), 'ctx', split_axis=0, concat_axis...]
    pallas_call x2, Pallas kernels: 2.7 us -> 1.48 us  [the longest x1 1.29 us: on_device(): pl.pallas_call(functools.partial(group_kernel, float(length), float(width...]
  transfers between devices with their start and end apart: 1 -> 0, of which waited for: 1 -> 0; matrix products, arithmetic and copies ran while one was open for 0% -> 0% of each run, Pallas kernels for 5% -> 0%
where the time goes in v4:
time: 41.1 us; the launch traced here: 40.8 us
  blocking collectives  34.8 us (85%)
  Pallas kernels  5.41 us (13%)
  between operations  0.65 us (2%)
    all_to_all x3, blocking collectives, exchange(): lax.all_to_all(table, 'ctx', split_axis=0, concat_axis=0, axis_index_grou...  34.8 us
    pallas_call x1, Pallas kernels, on_device(): pl.pallas_call(functools.partial(summary_kernel, float(length)), out_shap...  2.69 us
    pallas_call x1, Pallas kernels, on_device(): pl.pallas_call(functools.partial(group_kernel, float(length), float(width...  1.29 us
    pallas_call x1, Pallas kernels, on_device(): pl.pallas_call(functools.partial(output_kernel, float(length)), out_shape...  1.23 us

profile of v4, /device:TPU:24, one launch (start us, length us, event | category | flops | bytes accessed | tf_op | source)
XLA Modules:
  0.0 40.8 jit_solution(18162940348092541065)
XLA Ops:
  0.6 2.7 %chunk_summary.1 = (f32[192,128]{1,0:T(8,128)S(1)}, bf16[256,128]{1,0:T(8,128)(2,1)S(1)}, bf16[256,128]{1,0:T(8,128)(2,1)S(1)}, bf16[256,128]{1,0:T(8,128)(2,1)}...) custom-call(s32[1]{0:T(128)} %bitcast.index_ref, ...), custom_call_target="tpu_custom_call" | custom-call | tf_op jit(solution)/shard_map/chunk_summary/pallas_call | solution.py:281
  3.3 8.1 %all_to_all.15 = f32[4,48,128]{2,1,0:T(8,128)S(1)} all-to-all(f32[4,48,128]{2,1,0:T(8,128)S(1)} %bitcast.16), channel_id=1, replica_groups={{48,32,16,0},{112,96,80,64},{176,160,144,128},{240,224,208,192},{304,28..., dimensions={0} | all-to-all | bytes 196608 | tf_op jit(solution)/shard_map/all_to_all | solution.py:278
  11.4 1.3 %group_summary.1 = (bf16[384,128]{1,0:T(8,128)(2,1)S(1)}, f32[128,256]{1,0:T(8,128)S(1)}, f32[128,256]{1,0:T(8,128)S(1)}, f32[16,8,256]{2,1,0:T(8,128)S(1)}, f32...) custom-call(s32[1]{0:T(128)} %bitcast.index_ref, f32[192,128]{1,0:T(8,128)S(1)} %bitcast.11, ...), custom_call_target="tpu_custom_call" | custom-call | tf_op jit(solution)/shard_map/group_summary/pallas_call | solution.py:291
  12.7 19.3 %all_to_all.16 = bf16[8,48,128]{2,1,0:T(8,128)(2,1)S(1)} all-to-all(bf16[8,48,128]{2,1,0:T(8,128)(2,1)S(1)} %bitcast.17), channel_id=1, replica_groups={{320,256,192,128,64,0,448,384},{336,272,208,144,80,16,464,400},{352,288..., dimensions={0} | all-to-all | bytes 196608 | tf_op jit(solution)/shard_map/all_to_all | solution.py:278
  31.9 0.2 totals.1
  32.1 7.5 %all_to_all.17 = f32[4,32,128]{2,1,0:T(8,128)S(1)} all-to-all(f32[4,32,128]{2,1,0:T(8,128)S(1)} %bitcast.14), channel_id=1, replica_groups={{48,32,16,0},{112,96,80,64},{176,160,144,128},{240,224,208,192},{304,28..., dimensions={0} | all-to-all | bytes 131072 | tf_op jit(solution)/shard_map/all_to_all | solution.py:278
  39.6 1.2 %outputs.1 = (bf16[256,128]{1,0:T(8,128)(2,1)}, bf16[256,128]{1,0:T(8,128)(2,1)}, bf16[256,128]{1,0:T(8,128)(2,1)}, f32[16,256]{1,0:T(8,128)}, f32[16,256]{1,0:T(8,128)}) custom-call(s32[1]{0:T(128)} %bitcast.index_ref, f32[128,128]{1,0:T(8,128)S(1)} %bitcast.15, f32[128,256]{1,0:T(8,128)S(1)} %get-tuple-element.30.refs_0_, ...), custom_call_target="tpu_custom_call" | custom-call | tf_op jit(solution)/shard_map/outputs/pallas_call | solution.py:309

commit v5 on v4

--- a/solution.py
+++ b/solution.py
@@ -13,6 +13,8 @@
 BLOCK = 8
 LANES = 128
 NEAR = 4
+FLIP = 3
+STEPS = 32
 EARLY = 8
 MIB = 1024 * 1024
 
@@ -54,7 +56,7 @@
 
 
 def own_rates(length, near, index, log_ref):
-    block = near - 1 - lax.rem(index, near)
+    block = jnp.bitwise_xor(lax.rem(index, near), FLIP)
     logs = jnp.where(block >= 2, log_ref[:, LANES:], log_ref[:, :LANES])
     logs = jnp.where(lax.rem(block, 2) == 1, pltpu.roll(logs, LANES // 2, 1), logs)
     return jnp.exp(logs) / length
@@ -75,7 +77,8 @@
 
 
 def summary_kernel(length, index_ref, *refs):
-    sources, out_ref, held, (mixed, grad, sems) = refs[:6], refs[6], refs[7:13], refs[13:]
+    sources, out_ref, held, (mixed, grad, query_ref, sems) = refs[:6], refs[6], refs[7:12], refs[12:]
+    held = (*held[:2], query_ref, *held[2:])
     load_gates(sources, held, sems, mixed, grad)
     log_ref = held[4]
     width, channels = mixed.shape
@@ -84,8 +87,8 @@
 
     def step(block, carry):
         state, moment, res, rate, back, back_moment = carry
-        first = block * BLOCK
-        for row in range(BLOCK):
+        first = block * STEPS
+        for row in range(STEPS):
             mixed_row = mixed[pl.ds(first + row, 1), :]
             grad_row = grad[pl.ds(first + row, 1), :]
             late_row = grad[pl.ds(width - 1 - first - row, 1), :]
@@ -99,7 +102,7 @@
             back_moment = decay * back_moment + faded
         return state, moment, res, rate, back, back_moment
 
-    state, moment, res, rate, back, back_moment = lax.fori_loop(0, width // BLOCK, step, (zero,) * 6)
+    state, moment, res, rate, back, back_moment = lax.fori_loop(0, width // STEPS, step, (zero,) * 6)
     last = decay * state
     last_moment = decay * moment + last
     top = jnp.concatenate([last, back, last_moment], axis=0)
@@ -152,7 +155,8 @@
         local_part(length, mixed, grad, log_ref, residue_ref, *tables)
 
     fade = jnp.exp(-(own_rates(length, near, index_ref[0], log_ref) * width))
-    parts = [unpacked(parts_ref[at * rows : (at + 1) * rows, :]) for at in range(near - 1, -1, -1)]
+    places = [chunk ^ FLIP for chunk in range(near)]
+    parts = [unpacked(parts_ref[at * rows : (at + 1) * rows, :]) for at in places]
     whole, _, _ = joined(parts, fade, width)
     end, start, end_moment, start_moment, res, rate = whole
     top = jnp.concatenate([end, start, end_moment], axis=0)
@@ -178,17 +182,20 @@
         back = jnp.where(group == member, behind[member], back)
     states, backs = [], []
     for chunk in range(near):
-        block = parts_ref[(near - 1 - chunk) * rows : (near - chunk) * rows, :]
+        at = chunk ^ FLIP
+        block = parts_ref[at * rows : (at + 1) * rows, :]
         states.append(state)
         state = fade * state + block[:POLES]
     for chunk in range(near - 1, -1, -1):
-        block = parts_ref[(near - 1 - chunk) * rows : (near - chunk) * rows, :]
+        at = chunk ^ FLIP
+        block = parts_ref[at * rows : (at + 1) * rows, :]
         backs.append(back)
         back = fade * back + block[POLES : 2 * POLES]
     totals = jnp.concatenate(whole[4:], axis=0)
     rows = 2 * POLES
     for at in range(near):
-        entering = jnp.concatenate([states[near - 1 - at], backs[at]], axis=0)
+        chunk = at ^ FLIP
+        entering = jnp.concatenate([states[chunk], backs[near - 1 - chunk]], axis=0)
         out_ref[at * rows : (at + 1) * rows, :] = crossed(entering, totals)[0]
 
 
@@ -268,7 +275,7 @@
     near, far = NEAR, chunks // NEAR
     rows = 3 * POLES
     far_order = [(5 * far // 8 - place) % far for place in range(far)]
-    near_groups = [[group * near + near - 1 - place for place in range(near)] for group in range(far)]
+    near_groups = [[group * near + (place ^ FLIP) for place in range(near)] for group in range(far)]
     far_groups = [[group * near + member for group in far_order] for member in range(near)]
 
     def exchange(table, groups):
@@ -278,12 +285,12 @@
         table = lax.all_to_all(table, "ctx", split_axis=0, concat_axis=0, axis_index_groups=groups, tiled=True)
         return table.reshape(shape)
 
-    summary, key_gate, value_in, _, grad_output, logs, residues, mixed, grad = pl.pallas_call(
+    summary, key_gate, value_in, grad_output, logs, residues, mixed, grad = pl.pallas_call(
         functools.partial(summary_kernel, float(length)),
-        out_shape=(struct((near * rows, LANES), F32), gate, gate, gate, gate, pole, pole, turned, turned),
+        out_shape=(struct((near * rows, LANES), F32), gate, gate, gate, pole, pole, turned, turned),
         in_specs=[in_smem] + [in_hbm] * 6,
-        out_specs=[in_vmem] * 9,
-        scratch_shapes=[pltpu.SemaphoreType.DMA((6,))],
+        out_specs=[in_vmem] * 8,
+        scratch_shapes=[pltpu.VMEM(gate.shape, gate.dtype), pltpu.SemaphoreType.DMA((6,))],
         compiler_params=params,
         name="chunk_summary",
     )(index, *sources)

time: 41.1 us -> 40.5 us (0.985)
  Pallas kernels: 5.41 us -> 4.81 us
    pallas_call x1, Pallas kernels: 2.69 us -> 2.09 us  [on_device(): pl.pallas_call(functools.partial(summary_kernel, float(length)), out_shap...]
where the time goes in v5:
time: 40.5 us; the launch traced here: 40.2 us
  blocking collectives  34.8 us (86%)
  Pallas kernels  4.81 us (12%)
  between operations  0.65 us (2%)
    all_to_all x3, blocking collectives, exchange(): lax.all_to_all(table, 'ctx', split_axis=0, concat_axis=0, axis_index_grou...  34.8 us
    pallas_call x1, Pallas kernels, on_device(): pl.pallas_call(functools.partial(summary_kernel, float(length)), out_shap...  2.09 us
    pallas_call x1, Pallas kernels, on_device(): pl.pallas_call(functools.partial(group_kernel, float(length), float(width...  1.29 us
    pallas_call x1, Pallas kernels, on_device(): pl.pallas_call(functools.partial(output_kernel, float(length)), out_shape...  1.23 us

profile of v5, /device:TPU:24, one launch (start us, length us, event | category | flops | bytes accessed | tf_op | source)
XLA Modules:
  0.0 40.2 jit_solution(16086884976254973938)
XLA Ops:
  0.6 2.1 %chunk_summary.1 = (f32[192,128]{1,0:T(8,128)S(1)}, bf16[256,128]{1,0:T(8,128)(2,1)S(1)}, bf16[256,128]{1,0:T(8,128)(2,1)S(1)}, bf16[256,128]{1,0:T(8,128)(2,1)S...) custom-call(s32[1]{0:T(128)} %bitcast.index_ref, ...), custom_call_target="tpu_custom_call" | custom-call | tf_op jit(solution)/shard_map/chunk_summary/pallas_call | solution.py:288
  2.7 8.1 %all_to_all.15 = f32[4,48,128]{2,1,0:T(8,128)S(1)} all-to-all(f32[4,48,128]{2,1,0:T(8,128)S(1)} %bitcast.16), channel_id=1, replica_groups={{48,32,16,0},{112,96,80,64},{176,160,144,128},{240,224,208,192},{304,28..., dimensions={0} | all-to-all | bytes 196608 | tf_op jit(solution)/shard_map/all_to_all | solution.py:285
  10.8 1.3 %group_summary.1 = (bf16[384,128]{1,0:T(8,128)(2,1)S(1)}, f32[128,256]{1,0:T(8,128)S(1)}, f32[128,256]{1,0:T(8,128)S(1)}, f32[16,8,256]{2,1,0:T(8,128)S(1)}, f32...) custom-call(s32[1]{0:T(128)} %bitcast.index_ref, f32[192,128]{1,0:T(8,128)S(1)} %bitcast.11, ...), custom_call_target="tpu_custom_call" | custom-call | tf_op jit(solution)/shard_map/group_summary/pallas_call | solution.py:298
  12.1 19.3 %all_to_all.16 = bf16[8,48,128]{2,1,0:T(8,128)(2,1)S(1)} all-to-all(bf16[8,48,128]{2,1,0:T(8,128)(2,1)S(1)} %bitcast.17), channel_id=1, replica_groups={{320,256,192,128,64,0,448,384},{336,272,208,144,80,16,464,400},{352,288..., dimensions={0} | all-to-all | bytes 196608 | tf_op jit(solution)/shard_map/all_to_all | solution.py:285
  31.3 0.2 totals.1
  31.5 7.5 %all_to_all.17 = f32[4,32,128]{2,1,0:T(8,128)S(1)} all-to-all(f32[4,32,128]{2,1,0:T(8,128)S(1)} %bitcast.14), channel_id=1, replica_groups={{48,32,16,0},{112,96,80,64},{176,160,144,128},{240,224,208,192},{304,28..., dimensions={0} | all-to-all | bytes 131072 | tf_op jit(solution)/shard_map/all_to_all | solution.py:285
  39.0 1.2 %outputs.1 = (bf16[256,128]{1,0:T(8,128)(2,1)}, bf16[256,128]{1,0:T(8,128)(2,1)}, bf16[256,128]{1,0:T(8,128)(2,1)}, f32[16,256]{1,0:T(8,128)}, f32[16,256]{1,0:T(8,128)}) custom-call(s32[1]{0:T(128)} %bitcast.index_ref, f32[128,128]{1,0:T(8,128)S(1)} %bitcast.15, f32[128,256]{1,0:T(8,128)S(1)} %get-tuple-element.30.refs_0_, ...), custom_call_target="tpu_custom_call" | custom-call | tf_op jit(solution)/shard_map/outputs/pallas_call | solution.py:316

commit v6 on v5

--- a/solution.py
+++ b/solution.py
@@ -14,14 +14,14 @@
 LANES = 128
 NEAR = 4
 FLIP = 3
-STEPS = 32
+STEPS = 64
 EARLY = 8
 MIB = 1024 * 1024
 
 
 def gated(left_ref, right_ref):
     product = (left_ref[...].astype(F32) * right_ref[...].astype(F32)).astype(BF16)
-    return product.astype(F32).T
+    return product.T.astype(F32)
 
 
 def crossed(first, second):
@@ -113,7 +113,7 @@
         pair = crossed(top[:, here], low[:, here])
         for side in range(2):
             block = 2 * half + side
-            out_ref[block * rows : (block + 1) * rows, :] = pair[side]
+            out_ref[block * rows : (block + 1) * rows, :] = pair[side].astype(BF16)
 
 
 def local_part(length, mixed, grad, log_ref, residue_ref, conv_ref, back_ref, ahead_ref, behind_ref, fade_ref):
@@ -156,7 +156,7 @@
 
     fade = jnp.exp(-(own_rates(length, near, index_ref[0], log_ref) * width))
     places = [chunk ^ FLIP for chunk in range(near)]
-    parts = [unpacked(parts_ref[at * rows : (at + 1) * rows, :]) for at in places]
+    parts = [unpacked(parts_ref[at * rows : (at + 1) * rows, :].astype(F32)) for at in places]
     whole, _, _ = joined(parts, fade, width)
     end, start, end_moment, start_moment, res, rate = whole
     top = jnp.concatenate([end, start, end_moment], axis=0)
@@ -183,12 +183,12 @@
     states, backs = [], []
     for chunk in range(near):
         at = chunk ^ FLIP
-        block = parts_ref[at * rows : (at + 1) * rows, :]
+        block = parts_ref[at * rows : (at + 1) * rows, :].astype(F32)
         states.append(state)
         state = fade * state + block[:POLES]
     for chunk in range(near - 1, -1, -1):
         at = chunk ^ FLIP
-        block = parts_ref[at * rows : (at + 1) * rows, :]
+        block = parts_ref[at * rows : (at + 1) * rows, :].astype(F32)
         backs.append(back)
         back = fade * back + block[POLES : 2 * POLES]
     totals = jnp.concatenate(whole[4:], axis=0)
@@ -196,7 +196,7 @@
     for at in range(near):
         chunk = at ^ FLIP
         entering = jnp.concatenate([states[chunk], backs[near - 1 - chunk]], axis=0)
-        out_ref[at * rows : (at + 1) * rows, :] = crossed(entering, totals)[0]
+        out_ref[at * rows : (at + 1) * rows, :] = crossed(entering, totals)[0].astype(BF16)
 
 
 def output_kernel(length, index_ref, carried_ref, *refs):
@@ -214,7 +214,7 @@
     states = []
     for half in range(channels // LANES):
         here = slice(half * LANES, (half + 1) * LANES)
-        first, second = (carried_ref[at * size : (at + 1) * size, :] for at in (2 * half, 2 * half + 1))
+        first, second = (carried_ref[at * size : (at + 1) * size, :].astype(F32) for at in (2 * half, 2 * half + 1))
         entering, totals = crossed(first, second)
         states.append(entering)
         residue_out[:, here] = totals[:POLES] * (1.0 / length)
@@ -242,7 +242,7 @@
             for block in range(blocks):
                 total[block] = total[block] + term
                 term = term * fade
-        conv = jnp.concatenate(total, axis=0).T.astype(BF16).astype(F32)
+        conv = jnp.concatenate(total, axis=0).astype(BF16).T.astype(F32)
         query_out[here, :] = (out_grad_ref[here, :].astype(F32) * conv).astype(BF16)
         total = [back_ref[block * BLOCK : (block + 1) * BLOCK, here] for block in range(blocks)]
         for pole in range(POLES):
@@ -251,7 +251,7 @@
             for block in range(blocks - 1, -1, -1):
                 total[block] = total[block] + term
                 term = term * fade
-        back = jnp.concatenate(total, axis=0).T.astype(BF16).astype(F32)
+        back = jnp.concatenate(total, axis=0).astype(BF16).T.astype(F32)
         key_out[here, :] = (back * value_ref[here, :].astype(F32)).astype(BF16)
         value_out[here, :] = (back * key_ref[here, :].astype(F32)).astype(BF16)
 
@@ -287,7 +287,7 @@
 
     summary, key_gate, value_in, grad_output, logs, residues, mixed, grad = pl.pallas_call(
         functools.partial(summary_kernel, float(length)),
-        out_shape=(struct((near * rows, LANES), F32), gate, gate, gate, pole, pole, turned, turned),
+        out_shape=(struct((near * rows, LANES), BF16), gate, gate, gate, pole, pole, turned, turned),
         in_specs=[in_smem] + [in_hbm] * 6,
         out_specs=[in_vmem] * 8,
         scratch_shapes=[pltpu.VMEM(gate.shape, gate.dtype), pltpu.SemaphoreType.DMA((6,))],
@@ -306,7 +306,7 @@
     groups = exchange(group, far_groups)
     carried = pl.pallas_call(
         functools.partial(total_kernel, float(length), float(width), near, far_order),
-        out_shape=struct((near * 2 * POLES, LANES), F32),
+        out_shape=struct((near * 2 * POLES, LANES), BF16),
         in_specs=[in_smem, in_vmem, in_vmem, in_vmem],
         out_specs=in_vmem,
         compiler_params=params,

time: 40.5 us -> 39.8 us (0.983)
  blocking collectives: 34.8 us -> 34.3 us
    all_to_all x3, blocking collectives: 34.8 us -> 34.3 us  [exchange(): lax.all_to_all(table, 'ctx', split_axis=0, concat_axis=0, axis_index_grou...]
where the time goes in v6:
time: 39.8 us; the launch traced here: 39.6 us
  blocking collectives  34.3 us (86%)
  Pallas kernels  4.66 us (12%)
  between operations  0.65 us (2%)
    all_to_all x3, blocking collectives, exchange(): lax.all_to_all(table, 'ctx', split_axis=0, concat_axis=0, axis_index_grou...  34.3 us
    pallas_call x1, Pallas kernels, on_device(): pl.pallas_call(functools.partial(summary_kernel, float(length)), out_shap...  2.01 us
    pallas_call x1, Pallas kernels, on_device(): pl.pallas_call(functools.partial(group_kernel, float(length), float(width...  1.29 us
    pallas_call x1, Pallas kernels, on_device(): pl.pallas_call(functools.partial(output_kernel, float(length)), out_shape...  1.17 us

profile of v6, /device:TPU:24, one launch (start us, length us, event | category | flops | bytes accessed | tf_op | source)
XLA Modules:
  0.0 39.6 jit_solution(9121434452750999652)
XLA Ops:
  0.6 2.0 %chunk_summary.1 = (bf16[192,128]{1,0:T(8,128)(2,1)S(1)}, bf16[256,128]{1,0:T(8,128)(2,1)S(1)}, bf16[256,128]{1,0:T(8,128)(2,1)S(1)}, bf16[256,128]{1,0:T(8,128)...) custom-call(s32[1]{0:T(128)} %bitcast.index_ref, ...), custom_call_target="tpu_custom_call" | custom-call | tf_op jit(solution)/shard_map/chunk_summary/pallas_call | solution.py:288
  2.7 7.8 %all_to_all.15 = bf16[4,48,128]{2,1,0:T(8,128)(2,1)S(1)} all-to-all(bf16[4,48,128]{2,1,0:T(8,128)(2,1)S(1)} %bitcast.17), channel_id=1, replica_groups={{48,32,16,0},{112,96,80,64},{176,160,144,128},{240,224,208,192},{304,28..., dimensions={0} | all-to-all | bytes 98304 | tf_op jit(solution)/shard_map/all_to_all | solution.py:285
  10.4 1.3 %group_summary.1 = (bf16[384,128]{1,0:T(8,128)(2,1)S(1)}, f32[128,256]{1,0:T(8,128)S(1)}, f32[128,256]{1,0:T(8,128)S(1)}, f32[16,8,256]{2,1,0:T(8,128)S(1)}, f32...) custom-call(s32[1]{0:T(128)} %bitcast.index_ref, bf16[192,128]{1,0:T(8,128)(2,1)S(1)} %bitcast.11, ...), custom_call_target="tpu_custom_call" | custom-call | tf_op jit(solution)/shard_map/group_summary/pallas_call | solution.py:298
  11.7 19.3 %all_to_all.16 = bf16[8,48,128]{2,1,0:T(8,128)(2,1)S(1)} all-to-all(bf16[8,48,128]{2,1,0:T(8,128)(2,1)S(1)} %bitcast.16), channel_id=1, replica_groups={{320,256,192,128,64,0,448,384},{336,272,208,144,80,16,464,400},{352,288..., dimensions={0} | all-to-all | bytes 196608 | tf_op jit(solution)/shard_map/all_to_all | solution.py:285
  31.0 0.2 totals.1
  31.2 7.2 %all_to_all.17 = bf16[4,32,128]{2,1,0:T(8,128)(2,1)S(1)} all-to-all(bf16[4,32,128]{2,1,0:T(8,128)(2,1)S(1)} %bitcast.14), channel_id=1, replica_groups={{48,32,16,0},{112,96,80,64},{176,160,144,128},{240,224,208,192},{304,28..., dimensions={0} | all-to-all | bytes 65536 | tf_op jit(solution)/shard_map/all_to_all | solution.py:285
  38.4 1.2 %outputs.1 = (bf16[256,128]{1,0:T(8,128)(2,1)}, bf16[256,128]{1,0:T(8,128)(2,1)}, bf16[256,128]{1,0:T(8,128)(2,1)}, f32[16,256]{1,0:T(8,128)}, f32[16,256]{1,0:T(8,128)}) custom-call(s32[1]{0:T(128)} %bitcast.index_ref, bf16[128,128]{1,0:T(8,128)(2,1)S(1)} %bitcast.15, f32[128,256]{1,0:T(8,128)S(1)} %get-tuple-element.30.refs_0_, ...), custom_call_target="tpu_custom_call" | custom-call | tf_op jit(solution)/shard_map/outputs/pallas_call | solution.py:316

commit v7 on v6

--- a/solution.py
+++ b/solution.py
@@ -62,27 +62,44 @@
     return jnp.exp(logs) / length
 
 
-def load_gates(sources, held, sems, mixed, grad):
-    copies = [pltpu.make_async_copy(src, dst, sems.at[n]) for n, (src, dst) in enumerate(zip(sources, held))]
-    for copy in copies:
-        copy.start()
-    copies[0].wait()
-    copies[1].wait()
+def load_gates(length, sources, held, sems, mixed, grad):
+    pieces = 2
+    step = held[0].shape[0] // pieces
+
+    def copies_of(at):
+        if at >= 4:
+            return [pltpu.make_async_copy(sources[at], held[at], sems.at[at, 0])]
+        rows = [pl.ds(piece * step, step) for piece in range(pieces)]
+        return [
+            pltpu.make_async_copy(sources[at].at[row], held[at].at[row], sems.at[at, piece])
+            for piece, row in enumerate(rows)
+        ]
+
+    copies = [copies_of(at) for at in range(len(held))]
+    for group in (copies[4], *copies[:4], *copies[5:]):
+        for copy in group:
+            copy.start()
+
+    def arrived(*which):
+        for at in which:
+            for copy in copies[at]:
+                copy.wait()
+
+    arrived(4)
+    decay = jnp.exp(-(jnp.exp(held[4][...]) / length))
+    arrived(0, 1)
     mixed[...] = gated(held[0], held[1])
-    copies[2].wait()
-    copies[3].wait()
+    arrived(2, 3)
     grad[...] = gated(held[2], held[3])
-    for copy in copies[4:]:
-        copy.wait()
+    arrived(*range(5, len(held)))
+    return decay
 
 
 def summary_kernel(length, index_ref, *refs):
     sources, out_ref, held, (mixed, grad, query_ref, sems) = refs[:6], refs[6], refs[7:12], refs[12:]
     held = (*held[:2], query_ref, *held[2:])
-    load_gates(sources, held, sems, mixed, grad)
-    log_ref = held[4]
+    decay = load_gates(length, sources, held, sems, mixed, grad)
     width, channels = mixed.shape
-    decay = jnp.exp(-(jnp.exp(log_ref[...]) / length))
     zero = jnp.zeros((POLES, channels), F32)
 
     def step(block, carry):
@@ -290,7 +307,7 @@
         out_shape=(struct((near * rows, LANES), BF16), gate, gate, gate, pole, pole, turned, turned),
         in_specs=[in_smem] + [in_hbm] * 6,
         out_specs=[in_vmem] * 8,
-        scratch_shapes=[pltpu.VMEM(gate.shape, gate.dtype), pltpu.SemaphoreType.DMA((6,))],
+        scratch_shapes=[pltpu.VMEM(gate.shape, gate.dtype), pltpu.SemaphoreType.DMA((6, 2))],
         compiler_params=params,
         name="chunk_summary",
     )(index, *sources)

time: 39.8 us -> 39.9 us (level)
  no operation moved by 1% of the time
where the time goes in v7:
time: 39.9 us; the launch traced here: 39.6 us
  blocking collectives  34.3 us (86%)
  Pallas kernels  4.65 us (12%)
  between operations  0.65 us (2%)
    all_to_all x3, blocking collectives, exchange(): lax.all_to_all(table, 'ctx', split_axis=0, concat_axis=0, axis_index_grou...  34.3 us
    pallas_call x1, Pallas kernels, on_device(): pl.pallas_call(functools.partial(summary_kernel, float(length)), out_shap...  2 us
    pallas_call x1, Pallas kernels, on_device(): pl.pallas_call(functools.partial(group_kernel, float(length), float(width...  1.29 us
    pallas_call x1, Pallas kernels, on_device(): pl.pallas_call(functools.partial(output_kernel, float(length)), out_shape...  1.17 us

profile of v7, /device:TPU:24, one launch (start us, length us, event | category | flops | bytes accessed | tf_op | source)
XLA Modules:
  0.0 39.6 jit_solution(7527377565803253)
XLA Ops:
  0.6 2.0 %chunk_summary.1 = (bf16[192,128]{1,0:T(8,128)(2,1)S(1)}, bf16[256,128]{1,0:T(8,128)(2,1)S(1)}, bf16[256,128]{1,0:T(8,128)(2,1)S(1)}, bf16[256,128]{1,0:T(8,128)...) custom-call(s32[1]{0:T(128)} %bitcast.index_ref, ...), custom_call_target="tpu_custom_call" | custom-call | tf_op jit(solution)/shard_map/chunk_summary/pallas_call | solution.py:305
  2.6 7.8 %all_to_all.15 = bf16[4,48,128]{2,1,0:T(8,128)(2,1)S(1)} all-to-all(bf16[4,48,128]{2,1,0:T(8,128)(2,1)S(1)} %bitcast.17), channel_id=1, replica_groups={{48,32,16,0},{112,96,80,64},{176,160,144,128},{240,224,208,192},{304,28..., dimensions={0} | all-to-all | bytes 98304 | tf_op jit(solution)/shard_map/all_to_all | solution.py:302
  10.4 1.3 %group_summary.1 = (bf16[384,128]{1,0:T(8,128)(2,1)S(1)}, f32[128,256]{1,0:T(8,128)S(1)}, f32[128,256]{1,0:T(8,128)S(1)}, f32[16,8,256]{2,1,0:T(8,128)S(1)}, f32...) custom-call(s32[1]{0:T(128)} %bitcast.index_ref, bf16[192,128]{1,0:T(8,128)(2,1)S(1)} %bitcast.11, ...), custom_call_target="tpu_custom_call" | custom-call | tf_op jit(solution)/shard_map/group_summary/pallas_call | solution.py:315
  11.7 19.3 %all_to_all.16 = bf16[8,48,128]{2,1,0:T(8,128)(2,1)S(1)} all-to-all(bf16[8,48,128]{2,1,0:T(8,128)(2,1)S(1)} %bitcast.16), channel_id=1, replica_groups={{320,256,192,128,64,0,448,384},{336,272,208,144,80,16,464,400},{352,288..., dimensions={0} | all-to-all | bytes 196608 | tf_op jit(solution)/shard_map/all_to_all | solution.py:302
  31.0 0.2 totals.1
  31.2 7.2 %all_to_all.17 = bf16[4,32,128]{2,1,0:T(8,128)(2,1)S(1)} all-to-all(bf16[4,32,128]{2,1,0:T(8,128)(2,1)S(1)} %bitcast.14), channel_id=1, replica_groups={{48,32,16,0},{112,96,80,64},{176,160,144,128},{240,224,208,192},{304,28..., dimensions={0} | all-to-all | bytes 65536 | tf_op jit(solution)/shard_map/all_to_all | solution.py:302
  38.4 1.2 %outputs.1 = (bf16[256,128]{1,0:T(8,128)(2,1)}, bf16[256,128]{1,0:T(8,128)(2,1)}, bf16[256,128]{1,0:T(8,128)(2,1)}, f32[16,256]{1,0:T(8,128)}, f32[16,256]{1,0:T(8,128)}) custom-call(s32[1]{0:T(128)} %bitcast.index_ref, bf16[128,128]{1,0:T(8,128)(2,1)S(1)} %bitcast.15, f32[128,256]{1,0:T(8,128)S(1)} %get-tuple-element.30.refs_0_, ...), custom_call_target="tpu_custom_call" | custom-call | tf_op jit(solution)/shard_map/outputs/pallas_call | solution.py:333

commit v8 on v6

--- a/solution.py
+++ b/solution.py
@@ -15,6 +15,7 @@
 NEAR = 4
 FLIP = 3
 STEPS = 64
+CHAINS = 4
 EARLY = 8
 MIB = 1024 * 1024
 
@@ -235,25 +236,33 @@
     blocks = conv_ref.shape[0] // BLOCK
     for half, entering in enumerate(states):
         here = slice(half * LANES, (half + 1) * LANES)
-        total = [conv_ref[block * BLOCK : (block + 1) * BLOCK, here] for block in range(blocks)]
+        ahead = [conv_ref[block * BLOCK : (block + 1) * BLOCK, here] for block in range(blocks)]
         for pole in range(POLES):
             term = ahead_ref[pole, :, here] * entering[pole : pole + 1]
-            fade = fade_ref[pole : pole + 1, here]
-            for block in range(blocks):
-                total[block] = total[block] + term
-                term = term * fade
-        conv = jnp.concatenate(total, axis=0).astype(BF16).T.astype(F32)
+            spread(ahead, term, fade_ref[pole : pole + 1, here], range(blocks))
+        conv = jnp.concatenate(ahead, axis=0).astype(BF16).T.astype(F32)
         query_out[here, :] = (out_grad_ref[here, :].astype(F32) * conv).astype(BF16)
-        total = [back_ref[block * BLOCK : (block + 1) * BLOCK, here] for block in range(blocks)]
+        behind = [back_ref[block * BLOCK : (block + 1) * BLOCK, here] for block in range(blocks)]
         for pole in range(POLES):
             term = behind_ref[pole, :, here] * entering[POLES + pole : POLES + pole + 1]
-            fade = fade_ref[pole : pole + 1, here]
-            for block in range(blocks - 1, -1, -1):
-                total[block] = total[block] + term
-                term = term * fade
-        back = jnp.concatenate(total, axis=0).astype(BF16).T.astype(F32)
+            spread(behind, term, fade_ref[pole : pole + 1, here], range(blocks - 1, -1, -1))
+        back = jnp.concatenate(behind, axis=0).astype(BF16).T.astype(F32)
         key_out[here, :] = (back * value_ref[here, :].astype(F32)).astype(BF16)
         value_out[here, :] = (back * key_ref[here, :].astype(F32)).astype(BF16)
+
+
+def spread(total, term, fade, order):
+    terms = [term]
+    for _ in range(CHAINS - 1):
+        terms.append(terms[-1] * fade)
+    stride = fade
+    for _ in range(CHAINS.bit_length() - 1):
+        stride = stride * stride
+    for place, block in enumerate(order):
+        chain = place % CHAINS
+        total[block] = total[block] + terms[chain]
+        if place + CHAINS < len(order):
+            terms[chain] = terms[chain] * stride
 
 
 def on_device(query, key_gate, value_in, grad_output, residue, log_rate):

time: 39.8 us -> 39.8 us (level)
  no operation moved by 1% of the time
where the time goes in v8:
time: 39.8 us; the launch traced here: 39.6 us
  blocking collectives  34.3 us (86%)
  Pallas kernels  4.66 us (12%)
  between operations  0.65 us (2%)
    all_to_all x3, blocking collectives, exchange(): lax.all_to_all(table, 'ctx', split_axis=0, concat_axis=0, axis_index_grou...  34.3 us
    pallas_call x1, Pallas kernels, on_device(): pl.pallas_call(functools.partial(summary_kernel, float(length)), out_shap...  2.01 us
    pallas_call x1, Pallas kernels, on_device(): pl.pallas_call(functools.partial(group_kernel, float(length), float(width...  1.29 us
    pallas_call x1, Pallas kernels, on_device(): pl.pallas_call(functools.partial(output_kernel, float(length)), out_shape...  1.16 us

profile of v8, /device:TPU:24, one launch (start us, length us, event | category | flops | bytes accessed | tf_op | source)
XLA Modules:
  0.0 39.6 jit_solution(13023275107956884937)
XLA Ops:
  0.6 2.0 %chunk_summary.1 = (bf16[192,128]{1,0:T(8,128)(2,1)S(1)}, bf16[256,128]{1,0:T(8,128)(2,1)S(1)}, bf16[256,128]{1,0:T(8,128)(2,1)S(1)}, bf16[256,128]{1,0:T(8,128)...) custom-call(s32[1]{0:T(128)} %bitcast.index_ref, ...), custom_call_target="tpu_custom_call" | custom-call | tf_op jit(solution)/shard_map/chunk_summary/pallas_call | solution.py:297
  2.7 7.8 %all_to_all.15 = bf16[4,48,128]{2,1,0:T(8,128)(2,1)S(1)} all-to-all(bf16[4,48,128]{2,1,0:T(8,128)(2,1)S(1)} %bitcast.17), channel_id=1, replica_groups={{48,32,16,0},{112,96,80,64},{176,160,144,128},{240,224,208,192},{304,28..., dimensions={0} | all-to-all | bytes 98304 | tf_op jit(solution)/shard_map/all_to_all | solution.py:294
  10.4 1.3 %group_summary.1 = (bf16[384,128]{1,0:T(8,128)(2,1)S(1)}, f32[128,256]{1,0:T(8,128)S(1)}, f32[128,256]{1,0:T(8,128)S(1)}, f32[16,8,256]{2,1,0:T(8,128)S(1)}, f32...) custom-call(s32[1]{0:T(128)} %bitcast.index_ref, bf16[192,128]{1,0:T(8,128)(2,1)S(1)} %bitcast.11, ...), custom_call_target="tpu_custom_call" | custom-call | tf_op jit(solution)/shard_map/group_summary/pallas_call | solution.py:307
  11.7 19.3 %all_to_all.16 = bf16[8,48,128]{2,1,0:T(8,128)(2,1)S(1)} all-to-all(bf16[8,48,128]{2,1,0:T(8,128)(2,1)S(1)} %bitcast.16), channel_id=1, replica_groups={{320,256,192,128,64,0,448,384},{336,272,208,144,80,16,464,400},{352,288..., dimensions={0} | all-to-all | bytes 196608 | tf_op jit(solution)/shard_map/all_to_all | solution.py:294
  31.0 0.2 totals.1
  31.2 7.2 %all_to_all.17 = bf16[4,32,128]{2,1,0:T(8,128)(2,1)S(1)} all-to-all(bf16[4,32,128]{2,1,0:T(8,128)(2,1)S(1)} %bitcast.14), channel_id=1, replica_groups={{48,32,16,0},{112,96,80,64},{176,160,144,128},{240,224,208,192},{304,28..., dimensions={0} | all-to-all | bytes 65536 | tf_op jit(solution)/shard_map/all_to_all | solution.py:294
  38.4 1.2 %outputs.1 = (bf16[256,128]{1,0:T(8,128)(2,1)}, bf16[256,128]{1,0:T(8,128)(2,1)}, bf16[256,128]{1,0:T(8,128)(2,1)}, f32[16,256]{1,0:T(8,128)}, f32[16,256]{1,0:T(8,128)}) custom-call(s32[1]{0:T(128)} %bitcast.index_ref, bf16[128,128]{1,0:T(8,128)(2,1)S(1)} %bitcast.15, f32[128,256]{1,0:T(8,128)S(1)} %get-tuple-element.30.refs_0_, ...), custom_call_target="tpu_custom_call" | custom-call | tf_op jit(solution)/shard_map/outputs/pallas_call | solution.py:325

commit v9 on v6

--- a/solution.py
+++ b/solution.py
@@ -15,7 +15,7 @@
 NEAR = 4
 FLIP = 3
 STEPS = 64
-EARLY = 8
+EARLY = 4
 MIB = 1024 * 1024
 
 

time: 39.8 us -> 39.8 us (level)
  no operation moved by 1% of the time
where the time goes in v9:
time: 39.8 us; the launch traced here: 39.6 us
  blocking collectives  34.3 us (86%)
  Pallas kernels  4.66 us (12%)
  between operations  0.65 us (2%)
    all_to_all x3, blocking collectives, exchange(): lax.all_to_all(table, 'ctx', split_axis=0, concat_axis=0, axis_index_grou...  34.3 us
    pallas_call x1, Pallas kernels, on_device(): pl.pallas_call(functools.partial(summary_kernel, float(length)), out_shap...  2.01 us
    pallas_call x1, Pallas kernels, on_device(): pl.pallas_call(functools.partial(group_kernel, float(length), float(width...  1.29 us
    pallas_call x1, Pallas kernels, on_device(): pl.pallas_call(functools.partial(output_kernel, float(length)), out_shape...  1.17 us

profile of v9, /device:TPU:24, one launch (start us, length us, event | category | flops | bytes accessed | tf_op | source)
XLA Modules:
  0.0 39.6 jit_solution(18150077466257596727)
XLA Ops:
  0.6 2.0 %chunk_summary.1 = (bf16[192,128]{1,0:T(8,128)(2,1)S(1)}, bf16[256,128]{1,0:T(8,128)(2,1)S(1)}, bf16[256,128]{1,0:T(8,128)(2,1)S(1)}, bf16[256,128]{1,0:T(8,128)...) custom-call(s32[1]{0:T(128)} %bitcast.index_ref, ...), custom_call_target="tpu_custom_call" | custom-call | tf_op jit(solution)/shard_map/chunk_summary/pallas_call | solution.py:288
  2.7 7.8 %all_to_all.15 = bf16[4,48,128]{2,1,0:T(8,128)(2,1)S(1)} all-to-all(bf16[4,48,128]{2,1,0:T(8,128)(2,1)S(1)} %bitcast.17), channel_id=1, replica_groups={{48,32,16,0},{112,96,80,64},{176,160,144,128},{240,224,208,192},{304,28..., dimensions={0} | all-to-all | bytes 98304 | tf_op jit(solution)/shard_map/all_to_all | solution.py:285
  10.4 1.3 %group_summary.1 = (bf16[384,128]{1,0:T(8,128)(2,1)S(1)}, f32[128,256]{1,0:T(8,128)S(1)}, f32[128,256]{1,0:T(8,128)S(1)}, f32[16,8,256]{2,1,0:T(8,128)S(1)}, f32...) custom-call(s32[1]{0:T(128)} %bitcast.index_ref, bf16[192,128]{1,0:T(8,128)(2,1)S(1)} %bitcast.11, ...), custom_call_target="tpu_custom_call" | custom-call | tf_op jit(solution)/shard_map/group_summary/pallas_call | solution.py:298
  11.7 19.3 %all_to_all.16 = bf16[8,48,128]{2,1,0:T(8,128)(2,1)S(1)} all-to-all(bf16[8,48,128]{2,1,0:T(8,128)(2,1)S(1)} %bitcast.16), channel_id=1, replica_groups={{320,256,192,128,64,0,448,384},{336,272,208,144,80,16,464,400},{352,288..., dimensions={0} | all-to-all | bytes 196608 | tf_op jit(solution)/shard_map/all_to_all | solution.py:285
  31.0 0.2 totals.1
  31.2 7.2 %all_to_all.17 = bf16[4,32,128]{2,1,0:T(8,128)(2,1)S(1)} all-to-all(bf16[4,32,128]{2,1,0:T(8,128)(2,1)S(1)} %bitcast.14), channel_id=1, replica_groups={{48,32,16,0},{112,96,80,64},{176,160,144,128},{240,224,208,192},{304,28..., dimensions={0} | all-to-all | bytes 65536 | tf_op jit(solution)/shard_map/all_to_all | solution.py:285
  38.4 1.2 %outputs.1 = (bf16[256,128]{1,0:T(8,128)(2,1)}, bf16[256,128]{1,0:T(8,128)(2,1)}, bf16[256,128]{1,0:T(8,128)(2,1)}, f32[16,256]{1,0:T(8,128)}, f32[16,256]{1,0:T(8,128)}) custom-call(s32[1]{0:T(128)} %bitcast.index_ref, bf16[128,128]{1,0:T(8,128)(2,1)S(1)} %bitcast.15, f32[128,256]{1,0:T(8,128)S(1)} %get-tuple-element.30.refs_0_, ...), custom_call_target="tpu_custom_call" | custom-call | tf_op jit(solution)/shard_map/outputs/pallas_call | solution.py:316
